TPU v7x, 32 devices: a whole 2x2x4 slice. The times are simulated.
32 devices in a mesh: seg: 8 (over y, x, core), tok: 4 (over z).
Axes of the slice: x: 2, y: 2, z: 4, core: 2. Of those that a mesh axis runs over, the one named last changes fastest.
Arguments:
- incoming_items: bfloat16 [8, 1280, 1024], P('seg', 'tok'), may hold values from -6 to 6
- upstream_slope: bfloat16 [8, 1280, 1024], P('seg', 'tok'), may hold values from -6 to 6
- timemix_prior_entry: bfloat16 [8, 1024], P('seg'), may hold values from -6 to 6
- featmix_prior_entry: bfloat16 [8, 1024], P('seg'), may hold values from -6 to 6
- opening_dividend: float32 [8, 1024], P('seg', 'tok'), may hold values from -6 to 6
- opening_divisor: float32 [8, 1024], P('seg', 'tok'), may hold values from 0.5 to 4
- opening_power: float32 [8, 1024], P('seg', 'tok'), may hold values from -4 to 4
- normalize_scales: float32 [2, 1024], replicated, may hold values from 0.5 to 1.5
- normalize_shifts: float32 [2, 1024], replicated, may hold values from -1 to 1
- shift_blends: float32 [5, 1024], replicated, may hold values from 0.05 to 0.95
- logarithmic_fading_speed: float32 [1024], replicated, may hold values from -11.5 to -3
- present_reward: float32 [1024], replicated, may hold values from -1 to 1
- timemix_lookup_coeffs: bfloat16 [1024, 1024], replicated, may hold values from -0.1875 to 0.1875
- timemix_payload_coeffs: bfloat16 [1024, 1024], replicated, may hold values from -0.1875 to 0.1875
- timemix_accept_coeffs: bfloat16 [1024, 1024], replicated, may hold values from -0.1875 to 0.1875
- timemix_emit_coeffs: bfloat16 [1024, 1024], replicated, may hold values from -0.75 to 0.75
- featmix_lookup_coeffs: bfloat16 [1024, 4096], replicated, may hold values from -0.1875 to 0.1875
- featmix_payload_coeffs: bfloat16 [4096, 1024], replicated, may hold values from -0.09375 to 0.09375
- featmix_accept_coeffs: bfloat16 [1024, 1024], replicated, may hold values from -0.1875 to 0.1875
Outputs:
- layer_out: bfloat16 [8, 1280, 1024], P('seg', 'tok')
- token_grad: bfloat16 [8, 1280, 1024], P('seg', 'tok')
- final_num: float32 [8, 1024], P('seg', 'tok')
- final_den: float32 [8, 1024], P('seg', 'tok')
- final_top: float32 [8, 1024], P('seg', 'tok')
- gains_grad: float32 [2, 1024], P(None, ('seg', 'tok'))
- biases_grad: float32 [2, 1024], P(None, ('seg', 'tok'))
- mixes_grad: float32 [5, 1024], P(None, ('seg', 'tok'))
- decay_grad: float32 [1024], P(('seg', 'tok'))
- bonus_grad: float32 [1024], P(('seg', 'tok'))
- att_key_grad: float32 [1024, 1024], P(('seg', 'tok'))
- att_value_grad: float32 [1024, 1024], P(('seg', 'tok'))
- att_recept_grad: float32 [1024, 1024], P(('seg', 'tok'))
- att_out_grad: float32 [1024, 1024], P(('seg', 'tok'))
- ffn_key_grad: float32 [1024, 4096], P(('seg', 'tok'))
- ffn_value_grad: float32 [4096, 1024], P(('seg', 'tok'))
- ffn_recept_grad: float32 [1024, 1024], P(('seg', 'tok'))
All inputs are finite; a program needn't handle non-finite values.
Results may differ from a plain program's by a relative error of at most 0.024.
Values may be sent and summed in bfloat16 or wider, within the bound.
A program may use at most 192 MiB of HBM per device.

v0:
```python
from functools import partial

import jax
import jax.numpy as jnp
from jax import lax
from jax.sharding import PartitionSpec as P

EMBED_SIZE = 1024
FF = 4096
SPAN = 128


def passed_along(value, axis, steps):
    count = lax.axis_size(axis)
    first, last = (max(0, -steps), min(count, count - steps))
    return lax.ppermute(value, axis, [(source, source + steps) for source in range(first, last)])


def layer_norm(values, gain_row, bias_row):
    centre = values - jnp.mean(values, axis=-1, keepdims=True)
    spread = jnp.mean(centre * centre, axis=-1, keepdims=True)
    return centre * lax.rsqrt(spread + 1e-05) * gain_row + bias_row


def dense(left, right):
    return jnp.dot(left, right, preferred_element_type=jnp.float32)


def dense_back(left, right):
    return lax.dot_general(
        left, right, (((2,), (1,)), ((), ())), preferred_element_type=jnp.float32
    )


def outer_sum(left, right):
    return lax.dot_general(
        left, right, (((0, 1), (0, 1)), ((), ())), preferred_element_type=jnp.float32
    )


def blend(normed_low, before_low, weight_row):
    return normed_low * weight_row + before_low * (1.0 - weight_row)


def unmix(grads, weight_rows, normed_low, before_low):
    direct = grads[0] * weight_rows[0]
    across = grads[0] * (1.0 - weight_rows[0])
    for grad_item, weight_row in zip(grads[1:], weight_rows[1:]):
        direct = direct + grad_item * weight_row
        across = across + grad_item * (1.0 - weight_row)
    difference = normed_low - before_low
    totals = [jnp.sum(grad_item * difference, axis=(0, 1)) for grad_item in grads]
    return (direct, across.astype(jnp.bfloat16), totals)


def portion_iteration(lookup_series, payload_series, fading_portion, reward_portion, first_feature):
    seqs_here, length, portion_breadth = lookup_series.shape
    blocks = length // SPAN
    fading_multiplier = jnp.exp(fading_portion)
    steps = jnp.arange(SPAN, dtype=jnp.float32)
    lower = (steps[:, None] > steps[None, :]).astype(jnp.float32)
    place = steps[None, :, None]

    def block_step(handed_memory, stratum_arguments):
        numer, denom, stable = handed_memory
        lookup_tile_entries, value_blk = stratum_arguments
        lifted = lookup_tile_entries + place * fading_multiplier
        top = jnp.max(lifted, axis=1)
        scaled = jnp.exp(lifted - top[:, None, :])
        scaled_value = scaled * value_blk
        past_num = jnp.einsum("ts,nsc->ntc", lower, scaled_value, precision=lax.Precision.HIGHEST)
        past_den = jnp.einsum("ts,nsc->ntc", lower, scaled, precision=lax.Precision.HIGHEST)
        past_expo = top[:, None, :] - (place - 1.0) * fading_multiplier
        state_expo = stable[:, None, :] - place * fading_multiplier
        present_power = reward_portion + lookup_tile_entries
        peak = jnp.maximum(jnp.maximum(state_expo, present_power), past_expo)
        past_scale = jnp.exp(past_expo - peak)
        state_scale = jnp.exp(state_expo - peak)
        now_scale = jnp.exp(present_power - peak)
        numer_out = state_scale * numer[:, None, :] + past_scale * past_num + now_scale * value_blk
        denom_out = state_scale * denom[:, None, :] + past_scale * past_den + now_scale
        end_top = top - (SPAN - 1.0) * fading_multiplier
        faded = stable - SPAN * fading_multiplier
        peak_end = jnp.maximum(faded, end_top)
        keep_old = jnp.exp(faded - peak_end)
        keep_new = jnp.exp(end_top - peak_end)
        new_state = (
            keep_old * numer + keep_new * jnp.sum(scaled_value, axis=1),
            keep_old * denom + keep_new * jnp.sum(scaled, axis=1),
            peak_end,
        )
        return (new_state, numer_out / denom_out)

    key_blocks = lookup_series.reshape(seqs_here, blocks, SPAN, portion_breadth).transpose(
        1, 0, 2, 3
    )
    value_blocks = payload_series.reshape(seqs_here, blocks, SPAN, portion_breadth).transpose(
        1, 0, 2, 3
    )
    closing_memories, outputs = lax.scan(
        jax.checkpoint(block_step), first_feature, (key_blocks, value_blocks)
    )
    return (
        outputs.transpose(1, 0, 2, 3).reshape(seqs_here, length, portion_breadth),
        closing_memories,
    )


def rows_for(matrix, foremost_entries):
    return matrix.reshape(foremost_entries + (8, -1))


def portion_features(vector, foremost_entries):
    shaped = vector.reshape((vector.shape[0],) + foremost_entries + (-1,))
    return jnp.moveaxis(shaped, 0, len(foremost_entries))


def shards(
    incoming_items,
    upstream_slope,
    timemix_prior_entry,
    featmix_prior_entry,
    opening_dividend,
    opening_divisor,
    opening_power,
    normalize_scales,
    normalize_shifts,
    shift_blends,
    logarithmic_fading_speed,
    present_reward,
    timemix_lookup_coeffs,
    timemix_payload_coeffs,
    timemix_accept_coeffs,
    timemix_emit_coeffs,
    featmix_lookup_coeffs,
    featmix_payload_coeffs,
    featmix_accept_coeffs,
):
    at_start = lax.axis_index("tok") == 0
    inputs32 = incoming_items.astype(jnp.float32)
    normed32, norm_pull = jax.vjp(layer_norm, inputs32, normalize_scales[0], normalize_shifts[0])
    normed = normed32.astype(jnp.bfloat16)
    arrived = passed_along(normed[:, -1, :], "tok", 1)
    lead_row = jnp.where(at_start, timemix_prior_entry, arrived)
    before = jnp.concatenate([lead_row[:, None, :], normed[:, :-1, :]], axis=1)
    normed_low = normed.astype(jnp.float32)
    before_low = before.astype(jnp.float32)
    key_mix = blend(normed_low, before_low, shift_blends[0]).astype(jnp.bfloat16)
    value_mix = blend(normed_low, before_low, shift_blends[1]).astype(jnp.bfloat16)
    recept_mix = blend(normed_low, before_low, shift_blends[2]).astype(jnp.bfloat16)
    lookup_mapped = dense(key_mix, timemix_lookup_coeffs).astype(jnp.bfloat16)
    payload_mapped = dense(value_mix, timemix_payload_coeffs).astype(jnp.bfloat16)
    recept = jax.nn.sigmoid(dense(recept_mix, timemix_accept_coeffs))
    key_chan, value_chan = (
        lax.all_to_all(lookup_mapped, "tok", split_axis=2, concat_axis=1, tiled=True),
        lax.all_to_all(payload_mapped, "tok", split_axis=2, concat_axis=1, tiled=True),
    )
    portion_breadth = key_chan.shape[2]
    lateral_displacement = lax.axis_index("tok") * portion_breadth
    fading_portion = lax.dynamic_slice_in_dim(
        logarithmic_fading_speed, lateral_displacement, portion_breadth
    )
    reward_portion = lax.dynamic_slice_in_dim(present_reward, lateral_displacement, portion_breadth)
    first_feature = (opening_dividend, opening_divisor, opening_power)
    wkv_chan, recurrence_backward, closing_memories = jax.vjp(
        partial(portion_iteration, first_feature=first_feature),
        key_chan.astype(jnp.float32),
        value_chan.astype(jnp.float32),
        fading_portion,
        reward_portion,
        has_aux=True,
    )
    blended_entries = lax.all_to_all(
        wkv_chan.astype(jnp.bfloat16), "tok", split_axis=1, concat_axis=2, tiled=True
    )
    mixed_low = blended_entries.astype(jnp.float32)
    weighted = (recept * mixed_low).astype(jnp.bfloat16)
    middle = inputs32 + dense(weighted, timemix_emit_coeffs)
    normed_two32, norm_pull_two = jax.vjp(
        layer_norm, middle, normalize_scales[1], normalize_shifts[1]
    )
    normed_two = normed_two32.astype(jnp.bfloat16)
    arrived_two = passed_along(normed_two[:, -1, :], "tok", 1)
    lead_two = jnp.where(at_start, featmix_prior_entry, arrived_two)
    before_two = jnp.concatenate([lead_two[:, None, :], normed_two[:, :-1, :]], axis=1)
    normed_two_low = normed_two.astype(jnp.float32)
    before_two_low = before_two.astype(jnp.float32)
    key_two = blend(normed_two_low, before_two_low, shift_blends[3]).astype(jnp.bfloat16)
    recept_two = blend(normed_two_low, before_two_low, shift_blends[4]).astype(jnp.bfloat16)
    hidden = dense(key_two, featmix_lookup_coeffs)
    squared = jnp.square(jax.nn.relu(hidden)).astype(jnp.bfloat16)
    handed_memory = dense(squared, featmix_payload_coeffs)
    gate_two = jax.nn.sigmoid(dense(recept_two, featmix_accept_coeffs))
    layer_out = (middle + gate_two * handed_memory).astype(jnp.bfloat16)
    upstream = upstream_slope.astype(jnp.float32)
    grad_carried = (upstream * gate_two).astype(jnp.bfloat16)
    grad_gate = (upstream * handed_memory * gate_two * (1.0 - gate_two)).astype(jnp.bfloat16)
    grad_hidden = (
        dense_back(grad_carried, featmix_payload_coeffs) * 2.0 * jax.nn.relu(hidden)
    ).astype(jnp.bfloat16)
    grad_ffn_value = outer_sum(squared, grad_carried)
    grad_ffn_key = outer_sum(key_two, grad_hidden)
    grad_ffn_recept = outer_sum(recept_two, grad_gate)
    direct_two, across_two, mix_sums_two = unmix(
        (
            dense_back(grad_hidden, featmix_lookup_coeffs),
            dense_back(grad_gate, featmix_accept_coeffs),
        ),
        (shift_blends[3], shift_blends[4]),
        normed_two_low,
        before_two_low,
    )
    returned_two = passed_along(across_two[:, 0, :], "tok", -1)
    grad_normed_two = direct_two + jnp.concatenate(
        [across_two[:, 1:, :], returned_two[:, None, :]], axis=1
    ).astype(jnp.float32)
    grad_middle_norm, gain_two, bias_two = norm_pull_two(grad_normed_two)
    grad_middle = upstream + grad_middle_norm
    grad_branch = grad_middle.astype(jnp.bfloat16)
    grad_att_out = outer_sum(weighted, grad_branch)
    grad_weighted = dense_back(grad_branch, timemix_emit_coeffs)
    grad_mixed = (grad_weighted * recept).astype(jnp.bfloat16)
    grad_recept = (grad_weighted * mixed_low * recept * (1.0 - recept)).astype(jnp.bfloat16)
    grad_mixed_chan = lax.all_to_all(grad_mixed, "tok", split_axis=2, concat_axis=1, tiled=True)
    lookup_feature_slope, payload_feature_slope, fading_portion_slope, reward_portion_slope = (
        recurrence_backward(grad_mixed_chan.astype(jnp.float32))
    )
    grad_key, grad_value = (
        lax.all_to_all(
            lookup_feature_slope.astype(jnp.bfloat16),
            "tok",
            split_axis=1,
            concat_axis=2,
            tiled=True,
        ),
        lax.all_to_all(
            payload_feature_slope.astype(jnp.bfloat16),
            "tok",
            split_axis=1,
            concat_axis=2,
            tiled=True,
        ),
    )
    grad_att_key = outer_sum(key_mix, grad_key)
    grad_att_value = outer_sum(value_mix, grad_value)
    grad_att_recept = outer_sum(recept_mix, grad_recept)
    direct_one, across_one, mix_sums_one = unmix(
        (
            dense_back(grad_key, timemix_lookup_coeffs),
            dense_back(grad_value, timemix_payload_coeffs),
            dense_back(grad_recept, timemix_accept_coeffs),
        ),
        (shift_blends[0], shift_blends[1], shift_blends[2]),
        normed_low,
        before_low,
    )
    returned_one = passed_along(across_one[:, 0, :], "tok", -1)
    grad_normed = direct_one + jnp.concatenate(
        [across_one[:, 1:, :], returned_one[:, None, :]], axis=1
    ).astype(jnp.float32)
    grad_inputs, gain_one, bias_one = norm_pull(grad_normed)
    token_grad = (grad_middle + grad_inputs).astype(jnp.bfloat16)
    gain_grads = jnp.stack([gain_one, gain_two])
    bias_grads = jnp.stack([bias_one, bias_two])
    mix_grads = jnp.stack(mix_sums_one + mix_sums_two)
    decay_full = lax.dynamic_update_slice_in_dim(
        jnp.zeros(logarithmic_fading_speed.shape, jnp.float32),
        fading_portion_slope,
        lateral_displacement,
        0,
    )
    entire_reward = lax.dynamic_update_slice_in_dim(
        jnp.zeros(present_reward.shape, jnp.float32), reward_portion_slope, lateral_displacement, 0
    )
    count_seg = lax.axis_size("seg")
    count_tok = lax.axis_size("tok")
    foremost_entries = (count_seg * count_tok,)
    summed = (
        lax.psum_scatter(
            rows_for(grad_att_key, foremost_entries),
            ("seg", "tok"),
            scatter_dimension=0,
            tiled=True,
        ),
        lax.psum_scatter(
            rows_for(grad_att_value, foremost_entries),
            ("seg", "tok"),
            scatter_dimension=0,
            tiled=True,
        ),
        lax.psum_scatter(
            rows_for(grad_att_recept, foremost_entries),
            ("seg", "tok"),
            scatter_dimension=0,
            tiled=True,
        ),
        lax.psum_scatter(
            rows_for(grad_att_out, foremost_entries),
            ("seg", "tok"),
            scatter_dimension=0,
            tiled=True,
        ),
        lax.psum_scatter(
            rows_for(grad_ffn_key, foremost_entries),
            ("seg", "tok"),
            scatter_dimension=0,
            tiled=True,
        ),
        lax.psum_scatter(
            rows_for(grad_ffn_value, foremost_entries),
            ("seg", "tok"),
            scatter_dimension=0,
            tiled=True,
        ),
        lax.psum_scatter(
            rows_for(grad_ffn_recept, foremost_entries),
            ("seg", "tok"),
            scatter_dimension=0,
            tiled=True,
        ),
        lax.psum_scatter(
            portion_features(gain_grads, foremost_entries),
            ("seg", "tok"),
            scatter_dimension=0,
            tiled=True,
        ),
        lax.psum_scatter(
            portion_features(bias_grads, foremost_entries),
            ("seg", "tok"),
            scatter_dimension=0,
            tiled=True,
        ),
        lax.psum_scatter(
            portion_features(mix_grads, foremost_entries),
            ("seg", "tok"),
            scatter_dimension=0,
            tiled=True,
        ),
        lax.psum_scatter(
            portion_features(decay_full[None, :], foremost_entries),
            ("seg", "tok"),
            scatter_dimension=0,
            tiled=True,
        ),
        lax.psum_scatter(
            portion_features(entire_reward[None, :], foremost_entries),
            ("seg", "tok"),
            scatter_dimension=0,
            tiled=True,
        ),
    )
    (
        sum_key,
        sum_value,
        sum_recept,
        sum_out,
        sum_fkey,
        sum_fvalue,
        sum_frecept,
        sum_gain,
        sum_bias,
        sum_mix,
        sum_decay,
        reward_totalled,
    ) = summed
    return (
        layer_out,
        token_grad,
        closing_memories[0],
        closing_memories[1],
        closing_memories[2],
        sum_gain.reshape(sum_gain.shape[-2], sum_gain.shape[-1]),
        sum_bias.reshape(sum_bias.shape[-2], sum_bias.shape[-1]),
        sum_mix.reshape(sum_mix.shape[-2], sum_mix.shape[-1]),
        sum_decay.reshape(-1),
        reward_totalled.reshape(-1),
        sum_key.reshape(-1, EMBED_SIZE),
        sum_value.reshape(-1, EMBED_SIZE),
        sum_recept.reshape(-1, EMBED_SIZE),
        sum_out.reshape(-1, EMBED_SIZE),
        sum_fkey.reshape(-1, FF),
        sum_fvalue.reshape(-1, EMBED_SIZE),
        sum_frecept.reshape(-1, EMBED_SIZE),
    )


def solution(mesh):
    return jax.shard_map(
        shards,
        mesh=mesh,
        in_specs=(
            P("seg", "tok", None),
            P("seg", "tok", None),
            P("seg", None),
            P("seg", None),
            P("seg", "tok"),
            P("seg", "tok"),
            P("seg", "tok"),
            P(),
            P(),
            P(),
            P(),
            P(),
            P(),
            P(),
            P(),
            P(),
            P(),
            P(),
            P(),
        ),
        out_specs=(
            P("seg", "tok", None),
            P("seg", "tok", None),
            P("seg", "tok"),
            P("seg", "tok"),
            P("seg", "tok"),
            P(None, ("seg", "tok")),
            P(None, ("seg", "tok")),
            P(None, ("seg", "tok")),
            P(("seg", "tok")),
            P(("seg", "tok")),
            P(("seg", "tok"), None),
            P(("seg", "tok"), None),
            P(("seg", "tok"), None),
            P(("seg", "tok"), None),
            P(("seg", "tok"), None),
            P(("seg", "tok"), None),
            P(("seg", "tok"), None),
        ),
        check_vma=False,
    )
```

profile of v0, /device:TPU:0, one launch (start us, length us, event | category | flops | bytes accessed | tf_op | source)
XLA Modules:
  0.0 1699.0 jit_solution(6241449561331655630)
XLA Ops:
  23.3 7.4 reduce.109
  47.3 7.4 reduce.108
  90.7 42.8 %while.54 = (s32[]{:T(128)}, f32[1,256]{1,0:T(1,128)S(1)}, f32[1,256]{1,0:T(1,128)S(1)}, f32[1,256]{1,0:T(1,128)S(1)}, bf16[10,1,128,256]{3,2,0,1:T(8,128)(2,1)}...) while((s32[]{:T(128)}, f32[1,256]{1,0:T(1,128)S(1)}, ...), condition=%wide.region_6.7_spmd.clone.clone.clone, body=%wide.region_2.6_spmd.clone.clone.clone.sunk | while | flops 102271488 | bytes 2464941 | solution.py:100
  133.5 6.2 copy.160
  139.7 8.0 reduce.110
  152.4 16.1 all-to-all-done.2
  201.4 8.4 fusion.80
  209.9 6.6 fusion.176
  246.9 7.5 reduce.111
  271.5 17.5 %all-to-all-done.3 = bf16[4,2,40960]{2,1,0:T(2,128)(2,1)} async-done(((bf16[4,2,40960]{2,1,0:T(2,128)(2,1)}), bf16[4,2,40960]{2,1,0:T(2,128)(2,1)}, u32[]{:S(2)}, u32[]{:S(2)}) %all-to-all-start.3) | async-done | bytes 655392 | tf_op jit(solution)/shard_map/all_to_all | solution.py:224
  303.8 118.5 %while.53 = (s32[]{:T(128)}, f32[256]{0:T(256)}, f32[256]{0:T(256)}, f32[1,256]{1,0:T(1,128)}, f32[1,256]{1,0:T(1,128)}, /*index=5*/f32[1,256]{1,0:T(1,128)}, bf...) while((s32[]{:T(128)}, f32[256]{0:T(256)}, ...), condition=%wide.region_25.26_spmd.clone, body=%wide.region_11.25_spmd.clone.sunk | while | flops 207305600 | bytes 6589738 | solution.py:100
  428.6 8.8 reduce.113
  440.1 31.3 %all_to_all.66 = bf16[4,2,40960]{2,1,0:T(2,128)(2,1)} all-to-all(bf16[4,2,40960]{2,1,0:T(2,128)(2,1)} %reshape.2012), channel_id=1, replica_groups=mesh['seg'=8,'tok'=4] {'tok'}, dimensions={0} | all-to-all | bytes 1310720 | tf_op jit(solution)/shard_map/all_to_all | solution.py:229
  493.3 8.8 reduce.112
  504.8 30.8 %all_to_all.67 = bf16[4,2,40960]{2,1,0:T(2,128)(2,1)} all-to-all(bf16[4,2,40960]{2,1,0:T(2,128)(2,1)} %reshape.2010), channel_id=1, replica_groups=mesh['seg'=8,'tok'=4] {'tok'}, dimensions={0} | all-to-all | bytes 1310720 | tf_op jit(solution)/shard_map/all_to_all | solution.py:236
  551.3 13.3 fusion.122
  564.6 18.2 %reshape.1983 = f32[32,8,16384]{2,1,0:T(8,128)} reshape(f32[4096,1024]{1,0:T(8,128)} %fusion.122) | data formatting | bytes 33554432 | tf_op jit(solution)/shard_map/reshape | solution.py:110
  583.5 9.9 fusion.139
  593.4 20.4 %reshape.1981 = f32[32,8,16384]{2,1,0:T(8,128)} reshape(f32[1024,4096]{1,0:T(8,128)} %fusion.139) | data formatting | bytes 33554432 | tf_op jit(solution)/shard_map/reshape | solution.py:110
  642.9 50.4 %all-reduce.5 = (f32[32,2,32]{2,1,0:T(2,128)}, f32[32,2,32]{2,1,0:T(2,128)}, f32[32,5,32]{2,1,0:T(8,128)}, f32[32,1,32]{2,1,0:T(1,128)}, f32[32,1,32]{2,1,0:T(1,128)}) all-reduce(f32[32,2,32]{2,1,0:T(2,128)} %maximum_bitcast_fusion, f32[32,2,32]{2,1,0:T(2,128)} %maximum_bitcast_fusion.1, ...), channel_id=2, replica_groups=mesh['seg'=8,'tok'=4] {'seg','tok'}, use_global_device_ids=true, to_apply=%region_30.31.clone | all-reduce | flops 11264 | bytes 90112
  708.1 103.2 %reduce-scatter.8.cloned.1.call-done = f32[1,8,4096]{2,1,0:T(8,128)} async-done(((f32[32,8,4096]{2,1,0:T(8,128)}), f32[1,8,4096]{2,1,0:T(8,128)}) %reduce-scatter.8.cloned.1.call-update) | async-done | bytes 131088 | tf_op jit(solution)/shard_map/reduce_scatter | solution.py:279
  812.8 147.3 %reduce-scatter.10.cloned.1.call-done = f32[1,8,4096]{2,1,0:T(8,128)} async-done(((f32[32,8,4096]{2,1,0:T(8,128)}), f32[1,8,4096]{2,1,0:T(8,128)}) %reduce-scatter.10.cloned.1.call-update) | async-done | bytes 131088 | tf_op jit(solution)/shard_map/reduce_scatter | solution.py:285
  961.7 363.8 %reduce-scatter.18.cloned.1.call-done = f32[1,8,16384]{2,1,0:T(8,128)} async-done(((f32[32,8,16384]{2,1,0:T(8,128)}), f32[1,8,16384]{2,1,0:T(8,128)}) %reduce-scatter.18.cloned.1.call-update) | async-done | bytes 524304 | tf_op jit(solution)/shard_map/reduce_scatter | solution.py:309
  1327.5 362.5 %reduce-scatter.16.cloned.1.call-done = f32[1,8,16384]{2,1,0:T(8,128)} async-done(((f32[32,8,16384]{2,1,0:T(8,128)}), f32[1,8,16384]{2,1,0:T(8,128)}) %reduce-scatter.16.cloned.1.call-update) | async-done | bytes 524304 | tf_op jit(solution)/shard_map/reduce_scatter | solution.py:303
  (753 shorter events, 428.3 us)
Async XLA Ops:
  7.2 166.0 %copy-start = (bf16[1024,1024]{1,0:T(8,128)(2,1)S(1)}, bf16[1024,1024]{1,0:T(8,128)(2,1)}, u32[]{:S(2)}) copy-start(bf16[1024,1024]{1,0:T(8,128)(2,1)} %param.37) | copy-start | bytes 6291460
  11.0 6.2 collective-permute-start
  16.0 23.3 %copy-start.38 = (f32[1,1024]{1,0:T(1,128)}, f32[1,1024]{1,0:T(1,128)S(1)}, u32[]{:S(2)}) copy-start(f32[1,1024]{1,0:T(1,128)S(1)} %get-tuple-element.1028) | copy-start | bytes 12292
  16.0 245.2 %copy-start.34 = (f32[1,1024]{1,0:T(1,128)}, f32[1,1024]{1,0:T(1,128)S(1)}, u32[]{:S(2)}) copy-start(f32[1,1024]{1,0:T(1,128)S(1)} %get-tuple-element.1029) | copy-start | bytes 12292
  16.1 23.2 %copy-start.45 = (f32[1024]{0:T(1024)}, f32[1024]{0:T(1024)S(1)}, u32[]{:S(2)}) copy-start(f32[1024]{0:T(1024)S(1)} %get-tuple-element.1044) | copy-start | bytes 12292
  17.3 243.9 %copy-start.51 = (bf16[1,1,1024]{2,1,0:T(2,128)(2,1)}, bf16[1,1,1024]{2,1,0:T(2,128)(2,1)S(1)}, u32[]{:S(2)}) copy-start(bf16[1,1,1024]{2,1,0:T(2,128)(2,1)S(1)} %fusion.151) | copy-start | bytes 6148
  33.4 24.0 %all-to-all-start.1 = ((bf16[4,2,40960]{2,1,0:T(2,128)(2,1)}), bf16[4,2,40960]{2,1,0:T(2,128)(2,1)S(1)}, u32[]{:S(2)}, u32[]{:S(2)}) async-start(bf16[4,2,40960]{2,1,0:T(2,128)(2,1)} %reshape.2004), calls=%async_computation.1 | async-start | bytes 1310720 | tf_op jit(solution)/shard_map/all_to_all | solution.py:156
  57.4 21.3 %all-to-all-start = ((bf16[4,2,40960]{2,1,0:T(2,128)(2,1)}), bf16[4,2,40960]{2,1,0:T(2,128)(2,1)}, u32[]{:S(2)}, u32[]{:S(2)}) async-start(bf16[4,2,40960]{2,1,0:T(2,128)(2,1)} %reshape.2002), calls=%async_computation | async-start | bytes 1310720 | tf_op jit(solution)/shard_map/all_to_all | solution.py:155
  148.7 19.9 %all-to-all-start.2 = ((bf16[4,2,40960]{2,1,0:T(2,128)(2,1)}), bf16[4,2,40960]{2,1,0:T(2,128)(2,1)S(1)}, u32[]{:S(2)}, u32[]{:S(2)}) async-start(bf16[4,2,40960]{2,1,0:T(2,128)(2,1)} %reshape.2006), calls=%async_computation.2 | async-start | bytes 1310720 | tf_op jit(solution)/shard_map/all_to_all | solution.py:173
  152.2 551.1 %reduce-scatter.20.cloned.1.call-start = ((), (), s32[]{:S(2)}) async-start(), calls=%async_computation.19 | async-start | bytes 4325376 | tf_op jit(solution)/shard_map/reduce_scatter | solution.py:315
  152.4 108.8 %copy-start.41 = (f32[1024]{0:T(1024)}, f32[1024]{0:T(1024)S(1)}, u32[]{:S(2)}) copy-start(f32[1024]{0:T(1024)S(1)} %broadcast_subtract_fusion.4) | copy-start | bytes 12292
  177.5 2.7 collective-permute-start.1
  180.3 36.2 %copy-start.58 = (bf16[1,1,1024]{2,1,0:T(2,128)(2,1)}, bf16[1,1,1024]{2,1,0:T(2,128)(2,1)S(1)}, u32[]{:S(2)}) copy-start(bf16[1,1,1024]{2,1,0:T(2,128)(2,1)S(1)} %fusion.152) | copy-start | bytes 6148
  201.4 503.5 %reduce-scatter.14.cloned.1.call-start = ((), (), s32[]{:S(2)}) async-start(), calls=%async_computation.16 | async-start | bytes 4325376 | tf_op jit(solution)/shard_map/reduce_scatter | solution.py:297
  218.4 5.8 collective-permute-start.2
  256.9 32.1 %all-to-all-start.3 = ((bf16[4,2,40960]{2,1,0:T(2,128)(2,1)}), bf16[4,2,40960]{2,1,0:T(2,128)(2,1)}, u32[]{:S(2)}, u32[]{:S(2)}) async-start(bf16[4,2,40960]{2,1,0:T(2,128)(2,1)} %reshape.2008), calls=%async_computation.3 | async-start | bytes 1310720 | tf_op jit(solution)/shard_map/all_to_all | solution.py:224
  261.1 445.3 %reduce-scatter.12.cloned.1.call-start = ((), (), s32[]{:S(2)}) async-start(), calls=%async_computation.15 | async-start | bytes 4325376 | tf_op jit(solution)/shard_map/reduce_scatter | solution.py:291
  271.3 539.9 %reduce-scatter.8.cloned.1.call-start = ((), (), s32[]{:S(2)}) async-start(), calls=%async_computation.13 | async-start | bytes 4325376 | tf_op jit(solution)/shard_map/reduce_scatter | solution.py:279
  487.0 473.1 %reduce-scatter.10.cloned.1.call-start = ((), (), s32[]{:S(2)}) async-start(), calls=%async_computation.14 | async-start | bytes 4325376 | tf_op jit(solution)/shard_map/reduce_scatter | solution.py:285
  551.2 774.3 %reduce-scatter.18.cloned.1.call-start = ((), (), s32[]{:S(2)}) async-start(), calls=%async_computation.18 | async-start | bytes 17301504 | tf_op jit(solution)/shard_map/reduce_scatter | solution.py:309
  582.8 1107.2 %reduce-scatter.16.cloned.1.call-start = ((), (), s32[]{:S(2)}) async-start(), calls=%async_computation.17 | async-start | bytes 17301504 | tf_op jit(solution)/shard_map/reduce_scatter | solution.py:303
  626.2 5.8 collective-permute-start.3
  636.0 64.1 %copy-start.14 = (bf16[1,320,1024]{2,1,0:T(8,128)(2,1)S(1)}, bf16[1,320,1024]{2,1,0:T(8,128)(2,1)}, u32[]{:S(2)}) copy-start(bf16[1,320,1024]{2,1,0:T(8,128)(2,1)} %param.24) | copy-start | bytes 1966084
  636.0 64.1 %copy-start.57 = (f32[320]{0:T(512)S(1)}, f32[320]{0:T(512)}, u32[]{:S(2)}) copy-start(f32[320]{0:T(512)} %copy-done.55) | copy-start | bytes 3844
  (91 other events, 306.9 us)
Sparse Core Ops, SparseCore 0:
  201.5 153.8 reduce-scatter.19
  357.6 151.0 reduce-scatter.13
  510.9 151.8 reduce-scatter.11
  665.0 146.2 reduce-scatter.7
  813.4 146.7 reduce-scatter.9
  962.3 363.2 reduce-scatter.17
  1327.8 362.1 reduce-scatter.15
where the time goes:
time: 1710 us; the launch traced here: 1700 us
  waiting for transfers between devices  1020 us (60%)
  local copies, waits for them, and re-layouts  267 us (16%)
  other arithmetic  135 us (8%)
  matrix products  115 us (7%)
  blocking collectives  113 us (7%)
  starting transfers between devices  29.1 us (2%)
    reduce_scatter x1, waiting for transfers between devices, shards(): lax.psum_scatter(rows_for(grad_ffn_value, foremost_entries), ('seg', 'tok...  364 us
    reduce_scatter x1, waiting for transfers between devices, shards(): lax.psum_scatter(rows_for(grad_ffn_key, foremost_entries), ('seg', 'tok')...  363 us
    reduce_scatter x1, waiting for transfers between devices, shards(): lax.psum_scatter(rows_for(grad_att_value, foremost_entries), ('seg', 'tok...  147 us
    reduce_scatter x1, waiting for transfers between devices, shards(): lax.psum_scatter(rows_for(grad_att_key, foremost_entries), ('seg', 'tok')...  103 us
    reshape x7, local copies, waits for them, and re-layouts, rows_for(): return matrix.reshape(foremost_entries + (8, -1))  66.8 us
    unnamed x1, blocking collectives  50.4 us
    unnamed x12, other arithmetic  47.8 us
    unnamed x178, local copies, waits for them, and re-layouts  46.2 us
  transfers between devices with their start and end apart: 15, of which 11 were waited for; matrix products, arithmetic and copies ran while one was open for 23% of the time, Pallas kernels for 0%

commit v1 on v0

--- a/solution.py
+++ b/solution.py
@@ -3,11 +3,15 @@
 import jax
 import jax.numpy as jnp
 from jax import lax
+from jax.experimental import pallas as pl
+from jax.experimental.pallas import tpu as pltpu
 from jax.sharding import PartitionSpec as P
 
 EMBED_SIZE = 1024
 FF = 4096
 SPAN = 128
+VMEM_BYTES = 62 << 20
+MESH = pl.DeviceIdType.MESH
 
 
 def passed_along(value, axis, steps):
@@ -29,12 +33,6 @@
 def dense_back(left, right):
     return lax.dot_general(
         left, right, (((2,), (1,)), ((), ())), preferred_element_type=jnp.float32
-    )
-
-
-def outer_sum(left, right):
-    return lax.dot_general(
-        left, right, (((0, 1), (0, 1)), ((), ())), preferred_element_type=jnp.float32
     )
 
 
@@ -106,13 +104,364 @@
     )
 
 
-def rows_for(matrix, foremost_entries):
-    return matrix.reshape(foremost_entries + (8, -1))
-
-
-def portion_features(vector, foremost_entries):
-    shaped = vector.reshape((vector.shape[0],) + foremost_entries + (-1,))
-    return jnp.moveaxis(shaped, 0, len(foremost_entries))
+class Plan:
+    def __init__(self, count_seg, count_tok):
+        self.count_seg, self.count_tok = count_seg, count_tok
+        self.bits = count_seg.bit_length() - 1
+        self.seg_rows = EMBED_SIZE // count_seg
+        self.seg_rows_ff = FF // count_seg
+        self.low_bits = max(0, (128 // self.seg_rows).bit_length() - 1)
+        self.pair = self.low_bits
+        self.rest = [b for b in range(self.bits) if b != self.pair]
+        self.orders = (self.rest, self.rest[::-1])
+        self.stages = len(self.rest)
+        self.slots = 1 << self.stages
+        self.rows = self.seg_rows // count_tok
+        self.rows_ff = self.seg_rows_ff // count_tok
+        self.tok_here = self.rows % 16 == 0
+
+    def recv_offset(self, stage):
+        return self.slots - (self.slots >> stage)
+
+    def slot(self, order, relative):
+        total = 0
+        for place, bit in enumerate(order):
+            total = total + relative[bit] * (1 << (self.stages - 1 - place))
+        return total
+
+
+def bit_of(value, bit):
+    return lax.rem(lax.div(value, 1 << bit), 2)
+
+
+def flip(value, bit):
+    return value + (1 - 2 * bit_of(value, bit)) * (1 << bit)
+
+
+def seg_block(plan, seg, relative):
+    total = bit_of(seg, plan.pair) * (1 << plan.pair)
+    for bit, rel in relative.items():
+        own = bit_of(seg, bit)
+        total = total + (own + rel - 2 * own * rel) * (1 << bit)
+    return total
+
+
+def combos(bits):
+    for index in range(1 << len(bits)):
+        yield {bit: (index >> place) & 1 for place, bit in enumerate(bits)}
+
+
+class Wire:
+    def __init__(self, plan, seg, tok, own, recv, last, send_sem, recv_sem, far_send, far_recv):
+        self.plan, self.seg, self.tok = plan, seg, tok
+        self.own, self.recv, self.last = own, recv, last
+        self.send_sem, self.recv_sem = send_sem, recv_sem
+        self.far_send, self.far_recv = far_send, far_recv
+
+    def views(self, chunk, half):
+        kind, place = chunk[0], chunk[1]
+        pick = 0 if kind == "S" else 1
+        return (
+            self.own[pick].at[place, half],
+            self.recv[pick].at[place, half],
+            self.last[pick].at[place, half],
+        )
+
+    def copy(self, chunk, half, stage):
+        plan = self.plan
+        own, recv, _ = self.views(chunk, half)
+        size = plan.slots >> (stage + 1)
+        return pltpu.make_async_remote_copy(
+            src_ref=own.at[pl.ds(size, size)],
+            dst_ref=recv.at[pl.ds(plan.recv_offset(stage), size)],
+            send_sem=self.send_sem.at[chunk[2], half, stage],
+            recv_sem=self.recv_sem.at[chunk[2], half, stage],
+            device_id={"seg": flip(self.seg, plan.orders[half][stage])},
+            device_id_type=MESH,
+        )
+
+    def far_copy(self, chunk, half, step):
+        plan = self.plan
+        own, _, last = self.views(chunk, half)
+        rows = plan.rows if chunk[0] == "S" else plan.rows_ff
+        target = lax.rem(self.tok + step, plan.count_tok)
+        return pltpu.make_async_remote_copy(
+            src_ref=own.at[0, pl.ds(pl.multiple_of(target * rows, rows), rows)],
+            dst_ref=last.at[step - 1],
+            send_sem=self.far_send.at[chunk[2], half, step - 1],
+            recv_sem=self.far_recv.at[chunk[2], half, step - 1],
+            device_id={"tok": target},
+            device_id_type=MESH,
+        )
+
+    def start(self, chunk, stage):
+        plan = self.plan
+        for half in range(2):
+            if stage < plan.stages:
+                self.copy(chunk, half, stage).start()
+            elif plan.tok_here:
+                for step in range(1, plan.count_tok):
+                    self.far_copy(chunk, half, step).start()
+
+    def arrive(self, chunk, stage):
+        plan = self.plan
+        size = plan.slots >> (stage + 1)
+        for half in range(2):
+            self.copy(chunk, half, stage).wait()
+            own, recv, _ = self.views(chunk, half)
+            base = plan.recv_offset(stage)
+
+            @pl.loop(0, size)
+            def _(slot):
+                total = own[slot].astype(jnp.float32) + recv[base + slot].astype(jnp.float32)
+                own[slot] = total.astype(jnp.bfloat16)
+
+        self.start(chunk, stage + 1)
+
+    def finish(self, chunk, out_ref, column):
+        plan = self.plan
+        rows = plan.rows if chunk[0] == "S" else plan.rows_ff
+        for half in range(2):
+            own, _, last = self.views(chunk, half)
+            wide = own.shape[-1]
+            place = pl.ds(column + half * wide, wide)
+            if not plan.tok_here:
+                out_ref[:, place] = own[0].astype(jnp.float32)
+                continue
+            mine = pl.multiple_of(self.tok * rows, rows)
+            total = own[0, pl.ds(mine, rows)].astype(jnp.float32)
+            for step in range(1, plan.count_tok):
+                self.far_copy(chunk, half, step).wait()
+                total = total + last[step - 1].astype(jnp.float32)
+            out_ref[:, place] = total
+
+
+def greet(plan, seg, tok):
+    barrier = pltpu.get_barrier_semaphore()
+    for bit in range(plan.bits):
+        pl.semaphore_signal(
+            barrier, inc=1, device_id={"seg": flip(seg, bit)}, device_id_type=MESH
+        )
+    for step in range(1, plan.count_tok):
+        pl.semaphore_signal(
+            barrier,
+            inc=1,
+            device_id={"tok": lax.rem(tok + step, plan.count_tok)},
+            device_id_type=MESH,
+        )
+    pl.semaphore_wait(barrier, plan.bits + plan.count_tok - 1)
+
+
+def outer_chunk(plan, seg, chunk, wire, left, right, column):
+    low = range(plan.low_bits)
+    nsub = 1 << plan.low_bits
+    high = [b for b in plan.rest if b >= plan.low_bits]
+    wide = 512 if chunk[0] == "S" else 128
+    rows = plan.seg_rows if chunk[0] == "S" else plan.seg_rows_ff
+    for relative in combos(high):
+        block = seg_block(plan, seg, relative)
+        if chunk[0] == "S":
+            block = lax.div(block, nsub)
+            parts = [(rows * nsub, block, None)]
+        else:
+            parts = [(rows, block + sub, sub) for sub in range(nsub)]
+        for span, index, sub in parts:
+            start = pl.multiple_of(index * span, span)
+            taken = left[:, pl.ds(start, span)]
+            for half in range(2):
+                result = lax.dot_general(
+                    taken,
+                    right[:, pl.ds(column + half * wide, wide)],
+                    (((0,), (0,)), ((), ())),
+                    preferred_element_type=jnp.float32,
+                ).astype(jnp.bfloat16)
+                own, _, _ = wire.views(chunk, half)
+                for part in range(nsub) if sub is None else (sub,):
+                    full = dict(relative)
+                    for bit in low:
+                        mine = bit_of(seg, bit)
+                        want = (part >> bit) & 1
+                        full[bit] = mine + want - 2 * mine * want
+                    piece = result[part * rows : (part + 1) * rows] if sub is None else result
+                    own[plan.slot(plan.orders[half], full)] = piece
+
+
+CHUNKS = []
+for _j in range(4):
+    CHUNKS.append((("F", _j, len(CHUNKS)), 0, 256 * _j, "value", 256 * _j))
+CHUNKS.append((("S", 0, len(CHUNKS)), 1, 0, "frecept", 0))
+for _j in range(4):
+    CHUNKS.append((("S", 1 + _j, len(CHUNKS)), 2, 1024 * _j, "fkey", 1024 * _j))
+for _j, _name in enumerate(("out", "recept", "avalue", "akey")):
+    CHUNKS.append((("S", 5 + _j, len(CHUNKS)), 3 + _j, 0, _name, 0))
+NAMES = ("value", "frecept", "fkey", "out", "recept", "avalue", "akey")
+
+
+def gradient_kernel(plan, *refs):
+    lefts, refs = refs[:7], refs[7:]
+    rights, refs = refs[:7], refs[7:]
+    small_in, refs = refs[0], refs[1:]
+    outs, refs = dict(zip(NAMES, refs[:7])), refs[7:]
+    small_out, refs = refs[0], refs[1:]
+    left_cat, refs = refs[:7], refs[7:]
+    right_cat, refs = refs[:7], refs[7:]
+    own, recv, last, refs = refs[:2], refs[2:4], refs[4:6], refs[6:]
+    (small_recv, sems, far_sems, pair_sems, local_sems, small_sems) = refs
+    seg, tok = lax.axis_index("seg"), lax.axis_index("tok")
+    greet(plan, seg, tok)
+    wire = Wire(
+        plan, seg, tok, own, recv, last, sems.at[0], sems.at[1], far_sems.at[0], far_sems.at[1]
+    )
+    tokens = lefts[0].shape[0]
+    partner = flip(seg, plan.pair)
+    width = max(128, plan.seg_rows)
+    blocks = EMBED_SIZE // width
+    theirs = 1 - bit_of(seg, plan.pair)
+
+    def pair_copies(index):
+        wide = width * (lefts[index].shape[1] // EMBED_SIZE)
+        for pick in range(blocks // 2):
+            place = pl.ds(pl.multiple_of((2 * pick + theirs) * wide, wide), wide)
+            yield (
+                lefts[index].at[:, place],
+                left_cat[index].at[pl.ds(tokens, tokens), place],
+                pick,
+            )
+        yield (rights[index], right_cat[index].at[pl.ds(tokens, tokens)], blocks // 2)
+
+    def pair_copy(index, item):
+        source, target, number = item
+        return pltpu.make_async_remote_copy(
+            src_ref=source,
+            dst_ref=target,
+            send_sem=pair_sems.at[0, index, number],
+            recv_sem=pair_sems.at[1, index, number],
+            device_id={"seg": partner},
+            device_id_type=MESH,
+        )
+
+    def local_copies(index):
+        return (
+            pltpu.make_async_copy(
+                lefts[index], left_cat[index].at[pl.ds(0, tokens)], local_sems.at[0, index]
+            ),
+            pltpu.make_async_copy(
+                rights[index], right_cat[index].at[pl.ds(0, tokens)], local_sems.at[1, index]
+            ),
+        )
+
+    for index in range(7):
+        for item in pair_copies(index):
+            pair_copy(index, item).start()
+        for copy in local_copies(index):
+            copy.start()
+
+    ready = set()
+    for chunk, index, column, _, _ in CHUNKS:
+        if index not in ready:
+            ready.add(index)
+            for item in pair_copies(index):
+                pair_copy(index, item).wait()
+            for copy in local_copies(index):
+                copy.wait()
+        outer_chunk(plan, seg, chunk, wire, left_cat[index], right_cat[index], column)
+        wire.start(chunk, 0)
+
+    small_out[...] = small_in[...]
+    for bit in range(plan.bits):
+        copy = pltpu.make_async_remote_copy(
+            src_ref=small_out,
+            dst_ref=small_recv.at[bit],
+            send_sem=small_sems.at[0, bit],
+            recv_sem=small_sems.at[1, bit],
+            device_id={"seg": flip(seg, bit)},
+            device_id_type=MESH,
+        )
+        copy.start()
+        copy.wait()
+        small_out[...] += small_recv[bit]
+    copies = []
+    for step in range(1, plan.count_tok):
+        place = plan.bits + step - 1
+        copies.append(
+            pltpu.make_async_remote_copy(
+                src_ref=small_out,
+                dst_ref=small_recv.at[place],
+                send_sem=small_sems.at[0, place],
+                recv_sem=small_sems.at[1, place],
+                device_id={"tok": lax.rem(tok + step, plan.count_tok)},
+                device_id_type=MESH,
+            )
+        )
+        copies[-1].start()
+    for copy in copies:
+        copy.wait()
+    total = small_out[...]
+    for step in range(1, plan.count_tok):
+        total = total + small_recv[plan.bits + step - 1]
+    small_out[...] = total
+
+    count = len(CHUNKS)
+    for turn in range(count + plan.stages):
+        for stage in range(plan.stages):
+            if 0 <= turn - stage < count:
+                wire.arrive(CHUNKS[turn - stage][0], stage)
+        if turn >= plan.stages:
+            chunk, _, _, name, column = CHUNKS[turn - plan.stages]
+            wire.finish(chunk, outs[name], column)
+
+
+def gradient_sums(plan, lefts, rights, small):
+    tokens = lefts[0].shape[0]
+    rows = plan.rows if plan.tok_here else plan.seg_rows
+    rows_ff = plan.rows_ff if plan.tok_here else plan.seg_rows_ff
+    shapes = {name: (rows, EMBED_SIZE) for name in NAMES}
+    shapes["fkey"] = (rows, FF)
+    shapes["value"] = (rows_ff, EMBED_SIZE)
+    out_shape = [jax.ShapeDtypeStruct(shapes[name], jnp.float32) for name in NAMES]
+    out_shape.append(jax.ShapeDtypeStruct(small.shape, jnp.float32))
+    far = max(1, plan.count_tok - 1)
+    last_rows, last_rows_ff = (plan.rows, plan.rows_ff) if plan.tok_here else (16, 16)
+    low = jnp.bfloat16
+    halves = lambda kind, size, rows, wide: pltpu.VMEM((kind, 2, size, rows, wide), low)
+    got = pl.pallas_call(
+        partial(gradient_kernel, plan),
+        out_shape=out_shape,
+        in_specs=[pl.BlockSpec(memory_space=pl.ANY)] * 14
+        + [pl.BlockSpec(memory_space=pltpu.VMEM)],
+        out_specs=[pl.BlockSpec(memory_space=pltpu.VMEM)] * 8,
+        scratch_shapes=[pltpu.VMEM((2 * tokens, item.shape[1]), low) for item in lefts]
+        + [pltpu.VMEM((2 * tokens, item.shape[1]), low) for item in rights]
+        + [
+            halves(9, plan.slots, plan.seg_rows, 512),
+            halves(4, plan.slots, plan.seg_rows_ff, 128),
+            halves(9, plan.slots - 1, plan.seg_rows, 512),
+            halves(4, plan.slots - 1, plan.seg_rows_ff, 128),
+            halves(9, far, last_rows, 512),
+            halves(4, far, last_rows_ff, 128),
+            pltpu.VMEM((plan.bits + far,) + small.shape, jnp.float32),
+            pltpu.SemaphoreType.DMA((2, len(CHUNKS), 2, plan.stages)),
+            pltpu.SemaphoreType.DMA((2, len(CHUNKS), 2, far)),
+            pltpu.SemaphoreType.DMA((2, 7, EMBED_SIZE // max(128, plan.seg_rows) // 2 + 1)),
+            pltpu.SemaphoreType.DMA((2, 7)),
+            pltpu.SemaphoreType.DMA((2, plan.bits + far)),
+        ],
+        compiler_params=pltpu.CompilerParams(
+            collective_id=0, has_side_effects=True, vmem_limit_bytes=VMEM_BYTES
+        ),
+        cost_estimate=pl.CostEstimate(
+            flops=2 * tokens * 13 * EMBED_SIZE * EMBED_SIZE,
+            bytes_accessed=30 << 20,
+            transcendentals=0,
+        ),
+    )(*lefts, *rights, small)
+    sums = dict(zip(NAMES, got[:7]))
+    if not plan.tok_here:
+        sums = {
+            name: lax.psum_scatter(item, "tok", scatter_dimension=0, tiled=True)
+            for name, item in sums.items()
+        }
+    return sums, got[7]
 
 
 def shards(
@@ -198,9 +547,6 @@
     grad_hidden = (
         dense_back(grad_carried, featmix_payload_coeffs) * 2.0 * jax.nn.relu(hidden)
     ).astype(jnp.bfloat16)
-    grad_ffn_value = outer_sum(squared, grad_carried)
-    grad_ffn_key = outer_sum(key_two, grad_hidden)
-    grad_ffn_recept = outer_sum(recept_two, grad_gate)
     direct_two, across_two, mix_sums_two = unmix(
         (
             dense_back(grad_hidden, featmix_lookup_coeffs),
@@ -217,7 +563,6 @@
     grad_middle_norm, gain_two, bias_two = norm_pull_two(grad_normed_two)
     grad_middle = upstream + grad_middle_norm
     grad_branch = grad_middle.astype(jnp.bfloat16)
-    grad_att_out = outer_sum(weighted, grad_branch)
     grad_weighted = dense_back(grad_branch, timemix_emit_coeffs)
     grad_mixed = (grad_weighted * recept).astype(jnp.bfloat16)
     grad_recept = (grad_weighted * mixed_low * recept * (1.0 - recept)).astype(jnp.bfloat16)
@@ -241,9 +586,6 @@
             tiled=True,
         ),
     )
-    grad_att_key = outer_sum(key_mix, grad_key)
-    grad_att_value = outer_sum(value_mix, grad_value)
-    grad_att_recept = outer_sum(recept_mix, grad_recept)
     direct_one, across_one, mix_sums_one = unmix(
         (
             dense_back(grad_key, timemix_lookup_coeffs),
@@ -272,115 +614,50 @@
     entire_reward = lax.dynamic_update_slice_in_dim(
         jnp.zeros(present_reward.shape, jnp.float32), reward_portion_slope, lateral_displacement, 0
     )
-    count_seg = lax.axis_size("seg")
-    count_tok = lax.axis_size("tok")
-    foremost_entries = (count_seg * count_tok,)
-    summed = (
-        lax.psum_scatter(
-            rows_for(grad_att_key, foremost_entries),
-            ("seg", "tok"),
-            scatter_dimension=0,
-            tiled=True,
-        ),
-        lax.psum_scatter(
-            rows_for(grad_att_value, foremost_entries),
-            ("seg", "tok"),
-            scatter_dimension=0,
-            tiled=True,
-        ),
-        lax.psum_scatter(
-            rows_for(grad_att_recept, foremost_entries),
-            ("seg", "tok"),
-            scatter_dimension=0,
-            tiled=True,
-        ),
-        lax.psum_scatter(
-            rows_for(grad_att_out, foremost_entries),
-            ("seg", "tok"),
-            scatter_dimension=0,
-            tiled=True,
-        ),
-        lax.psum_scatter(
-            rows_for(grad_ffn_key, foremost_entries),
-            ("seg", "tok"),
-            scatter_dimension=0,
-            tiled=True,
-        ),
-        lax.psum_scatter(
-            rows_for(grad_ffn_value, foremost_entries),
-            ("seg", "tok"),
-            scatter_dimension=0,
-            tiled=True,
-        ),
-        lax.psum_scatter(
-            rows_for(grad_ffn_recept, foremost_entries),
-            ("seg", "tok"),
-            scatter_dimension=0,
-            tiled=True,
-        ),
-        lax.psum_scatter(
-            portion_features(gain_grads, foremost_entries),
-            ("seg", "tok"),
-            scatter_dimension=0,
-            tiled=True,
-        ),
-        lax.psum_scatter(
-            portion_features(bias_grads, foremost_entries),
-            ("seg", "tok"),
-            scatter_dimension=0,
-            tiled=True,
-        ),
-        lax.psum_scatter(
-            portion_features(mix_grads, foremost_entries),
-            ("seg", "tok"),
-            scatter_dimension=0,
-            tiled=True,
-        ),
-        lax.psum_scatter(
-            portion_features(decay_full[None, :], foremost_entries),
-            ("seg", "tok"),
-            scatter_dimension=0,
-            tiled=True,
-        ),
-        lax.psum_scatter(
-            portion_features(entire_reward[None, :], foremost_entries),
-            ("seg", "tok"),
-            scatter_dimension=0,
-            tiled=True,
-        ),
-    )
-    (
-        sum_key,
-        sum_value,
-        sum_recept,
-        sum_out,
-        sum_fkey,
-        sum_fvalue,
-        sum_frecept,
-        sum_gain,
-        sum_bias,
-        sum_mix,
-        sum_decay,
-        reward_totalled,
-    ) = summed
+    plan = Plan(lax.axis_size("seg"), lax.axis_size("tok"))
+    flat = lambda item: item[0]
+    small = jnp.concatenate(
+        [gain_grads, bias_grads, mix_grads, decay_full[None], entire_reward[None]]
+        + [jnp.zeros((5, EMBED_SIZE), jnp.float32)]
+    )
+    sums, small = gradient_sums(
+        plan,
+        [flat(x) for x in (squared, recept_two, key_two, weighted, recept_mix, value_mix, key_mix)],
+        [
+            flat(x)
+            for x in (
+                grad_carried,
+                grad_gate,
+                grad_hidden,
+                grad_branch,
+                grad_recept,
+                grad_value,
+                grad_key,
+            )
+        ],
+        small,
+    )
+    share = EMBED_SIZE // (plan.count_seg * plan.count_tok)
+    place = (lax.axis_index("seg") * plan.count_tok + lax.axis_index("tok")) * share
+    small = lax.dynamic_slice_in_dim(small, place, share, 1)
     return (
         layer_out,
         token_grad,
         closing_memories[0],
         closing_memories[1],
         closing_memories[2],
-        sum_gain.reshape(sum_gain.shape[-2], sum_gain.shape[-1]),
-        sum_bias.reshape(sum_bias.shape[-2], sum_bias.shape[-1]),
-        sum_mix.reshape(sum_mix.shape[-2], sum_mix.shape[-1]),
-        sum_decay.reshape(-1),
-        reward_totalled.reshape(-1),
-        sum_key.reshape(-1, EMBED_SIZE),
-        sum_value.reshape(-1, EMBED_SIZE),
-        sum_recept.reshape(-1, EMBED_SIZE),
-        sum_out.reshape(-1, EMBED_SIZE),
-        sum_fkey.reshape(-1, FF),
-        sum_fvalue.reshape(-1, EMBED_SIZE),
-        sum_frecept.reshape(-1, EMBED_SIZE),
+        small[0:2],
+        small[2:4],
+        small[4:9],
+        small[9],
+        small[10],
+        sums["akey"],
+        sums["avalue"],
+        sums["recept"],
+        sums["out"],
+        sums["fkey"],
+        sums["value"],
+        sums["frecept"],
     )
 
 

time: 1710 us -> 543 us (0.32)
  waiting for transfers between devices: 1020 us -> 42.2 us
  Pallas kernels: 0 us -> 175 us
  local copies, waits for them, and re-layouts: 267 us -> 124 us
  blocking collectives: 113 us -> 19.2 us
  other arithmetic: 135 us -> 75.1 us
  matrix products: 115 us -> 60.7 us
    reduce_scatter x7 -> x0, waiting for transfers between devices: 977 us -> none  [the longest x1 364 us: shards(): lax.psum_scatter(rows_for(grad_ffn_value, foremost_entries), ('seg', 'tok...]
    pallas_call x0 -> x1, Pallas kernels: none -> 175 us  [gradient_sums(): pl.pallas_call(partial(gradient_kernel, plan), out_shape=out_shape, in_sp...]
    reshape x19 -> x0, local copies, waits for them, and re-layouts: 84.8 us -> none  [the longest x7 66.8 us: rows_for(): return matrix.reshape(foremost_entries + (8, -1))]
    unnamed x1 -> x0, blocking collectives: 50.4 us -> none
    all_to_all x2 -> x1, blocking collectives: 62.2 us -> 19.2 us  [shards(): lax.all_to_all(wkv_chan.astype(jnp.bfloat16), 'tok', split_axis=1, concat...]
    dot_general x7 -> x0, matrix products: 41.1 us -> none  [outer_sum(): lax.dot_general(left, right, (((0, 1), (0, 1)), ((), ())), preferred_elem...]
    dynamic_update_slice x40, local copies, waits for them, and re-layouts: 18.8 us -> 1.4 us  [portion_iteration(): lax.scan(jax.checkpoint(block_step), first_feature, (key_blocks, value_bl...]
    unnamed x178 -> x121, local copies, waits for them, and re-layouts: 46.2 us -> 36.2 us
  transfers between devices with their start and end apart: 15 -> 9, of which waited for: 11 -> 8; matrix products, arithmetic and copies ran while one was open for 23% -> 8% of each run, Pallas kernels for 0% -> 0%
where the time goes in v1:
time: 543 us; the launch traced here: 535 us
  Pallas kernels  175 us (32%)
  local copies, waits for them, and re-layouts  124 us (23%)
  other arithmetic  75.1 us (14%)
  matrix products  60.7 us (11%)
  waiting for transfers between devices  42.2 us (8%)
  starting transfers between devices  34.2 us (6%)
  blocking collectives  19.2 us (4%)
    pallas_call x1, Pallas kernels, gradient_sums(): pl.pallas_call(partial(gradient_kernel, plan), out_shape=out_shape, in_sp...  175 us
    unnamed x13, other arithmetic  40.3 us
    unnamed x121, local copies, waits for them, and re-layouts  36.2 us
    dot_general x7, matrix products, dense_back(): lax.dot_general(left, right, (((2,), (1,)), ((), ())), preferred_element_...  20 us
    squeeze x40, local copies, waits for them, and re-layouts, portion_iteration(): lax.scan(jax.checkpoint(block_step), first_feature, (key_blocks, value_bl...  19.3 us
    all_to_all x1, blocking collectives, shards(): lax.all_to_all(wkv_chan.astype(jnp.bfloat16), 'tok', split_axis=1, concat...  19.2 us
    dot_general x7, matrix products, dense(): return jnp.dot(left, right, preferred_element_type=jnp.float32)  17 us
    all_to_all x1, waiting for transfers between devices, shards(): lax.all_to_all(grad_mixed, 'tok', split_axis=2, concat_axis=1, tiled=True)  14.1 us
  transfers between devices with their start and end apart: 9, of which 8 were waited for; matrix products, arithmetic and copies ran while one was open for 8% of the time, Pallas kernels for 0%

profile of v1, /device:TPU:0, one launch (start us, length us, event | category | flops | bytes accessed | tf_op | source)
XLA Modules:
  0.0 535.2 jit_solution(17022498850780798398)
XLA Ops:
  3.9 4.9 collective-permute-start
  17.7 6.6 %reduce.108 = bf16[1024,320]{1,0:T(8,128)(2,1)S(1)} reduce(bf16[1024,1,320]{2,1,0:T(2,128)(2,1)} %bitcast.520, bf16[]{:T(256)} %broadcast.1178), dimensions={1}, to_apply=%bitcast.345.reduce_sub_computation | reduce | bytes 1310722
  25.9 6.0 %all-to-all-start = ((bf16[4,2,40960]{2,1,0:T(2,128)(2,1)}), bf16[4,2,40960]{2,1,0:T(2,128)(2,1)S(1)}, u32[]{:S(2)}, u32[]{:S(2)}) async-start(bf16[4,2,40960]{2,1,0:T(2,128)(2,1)} %reshape.1895), calls=%async_computation | async-start | bytes 1310720 | tf_op jit(solution)/shard_map/all_to_all | solution.py:504
  37.4 6.6 %reduce.109 = bf16[1024,320]{1,0:T(8,128)(2,1)S(1)} reduce(bf16[1024,1,320]{2,1,0:T(2,128)(2,1)} %bitcast.521, bf16[]{:T(256)} %broadcast.1178), dimensions={1}, to_apply=%bitcast.347.reduce_sub_computation | reduce | bytes 1310722
  48.1 4.7 all-to-all-start.1
  62.4 7.2 %all-to-all-done.1 = bf16[4,2,40960]{2,1,0:T(2,128)(2,1)} async-done(((bf16[4,2,40960]{2,1,0:T(2,128)(2,1)}), bf16[4,2,40960]{2,1,0:T(2,128)(2,1)}, u32[]{:S(2)}, u32[]{:S(2)}) %all-to-all-start.1) | async-done | bytes 655392 | tf_op jit(solution)/shard_map/all_to_all | solution.py:505
  79.2 25.8 %while.54 = (s32[]{:T(128)}, f32[1,256]{1,0:T(1,128)S(1)}, f32[1,256]{1,0:T(1,128)S(1)}, f32[1,256]{1,0:T(1,128)S(1)}, bf16[10,1,128,256]{3,2,0,1:T(8,128)(2,1)S...) while((s32[]{:T(128)}, f32[1,256]{1,0:T(1,128)S(1)}, ...), condition=%wide.region_6.7_spmd.clone.clone.clone, body=%wide.region_2.6_spmd.clone.clone.clone.sunk | while | flops 102271488 | bytes 2464933 | solution.py:98
  105.0 7.4 %copy.149 = bf16[1,1280,256]{2,0,1:T(2,128)(2,1)S(1)} copy(bf16[1,1280,256]{2,1,0:T(8,128)(2,1)S(1)} %bitcast.553) | data formatting | bytes 1310720 | tf_op jit(solution)/shard_map/convert_element_type | solution.py:523
  112.4 6.9 %reduce.110 = bf16[1280,256]{1,0:T(8,128)(2,1)S(1)} reduce(bf16[1280,1,256]{2,1,0:T(2,128)(2,1)S(1)} %bitcast.535, bf16[]{:T(256)} %broadcast.1178), dimensions={1}, to_apply=%bitcast.401.reduce_sub_computation | reduce | bytes 1310722
  119.5 19.2 %all_to_all.66 = bf16[4,2,40960]{2,1,0:T(2,128)(2,1)S(1)} all-to-all(bf16[4,2,40960]{2,1,0:T(2,128)(2,1)S(1)} %reshape.1899), channel_id=1, replica_groups=mesh['seg'=8,'tok'=4] {'tok'}, dimensions={0} | all-to-all | bytes 1310720 | tf_op jit(solution)/shard_map/all_to_all | solution.py:522
  154.4 4.8 fusion.154
  161.7 8.3 %fusion.80.refs_9_ = bf16[320,4096]{1,0:T(8,128)(2,1)} fusion(f32[320,4096]{1,0:T(8,128)S(1)} %get-tuple-element.1030, bf16[320,1024]{1,0:T(8,128)(2,1)} %get-tuple-element.1006.refs_7_, bf16[4096,1024]{1,0:T(8,128)(2,1)} %param.40), kind=kOutput, calls=%fused_computation.156 | convolution fusion | flops 2688286720 | bytes 16908288 | tf_op jit(solution)/shard_map/dot_general | solution.py:34
  170.0 6.2 %fusion.155 = f32[320,1024]{1,0:T(8,128)S(1)} fusion(bf16[320,4096]{1,0:T(8,128)(2,1)} %fusion.80.refs_9_, bf16[1024,4096]{1,0:T(8,128)(2,1)} %param.39), kind=kOutput, calls=%fused_computation.310 | convolution fusion | flops 2684354560 | bytes 12320768 | tf_op jit(solution)/shard_map/dot_general | solution.py:34
  191.9 6.6 %reduce.111 = bf16[1024,320]{1,0:T(8,128)(2,1)S(1)} reduce(bf16[1024,1,320]{2,1,0:T(2,128)(2,1)} %bitcast.522, bf16[]{:T(256)} %broadcast.1178), dimensions={1}, to_apply=%bitcast.351.reduce_sub_computation | reduce | bytes 1310722
  203.8 14.1 %all-to-all-done.3 = bf16[4,2,40960]{2,1,0:T(2,128)(2,1)S(1)} async-done(((bf16[4,2,40960]{2,1,0:T(2,128)(2,1)}), bf16[4,2,40960]{2,1,0:T(2,128)(2,1)S(1)}, u32[]{:S(2)}, u32[]{:S(2)}) %all-to-all-start.3) | async-done | bytes 655392 | tf_op jit(solution)/shard_map/all_to_all | solution.py:569
  224.7 4.8 copy.107
  229.6 46.9 %while.53 = (s32[]{:T(128)}, f32[256]{0:T(256)S(1)}, f32[256]{0:T(256)S(1)}, f32[1,256]{1,0:T(1,128)S(1)}, f32[1,256]{1,0:T(1,128)S(1)}, /*index=5*/f32[1,256]{1...) while((s32[]{:T(128)}, f32[256]{0:T(256)S(1)}, ...), condition=%wide.region_25.26_spmd.clone, body=%wide.region_11.25_spmd.clone.sunk | while | flops 207305600 | bytes 6581482 | solution.py:98
  277.4 7.3 %copy.148 = bf16[1,1280,256]{2,0,1:T(2,128)(2,1)S(1)} copy(bf16[1,1280,256]{2,1,0:T(8,128)(2,1)S(1)} %bitcast.544) | data formatting | bytes 1310720 | tf_op jit(solution)/shard_map/convert_element_type | solution.py:575
  284.7 6.9 %reduce.113 = bf16[1280,256]{1,0:T(8,128)(2,1)S(1)} reduce(bf16[1280,1,256]{2,1,0:T(2,128)(2,1)S(1)} %bitcast.537, bf16[]{:T(256)} %broadcast.1178), dimensions={1}, to_apply=%bitcast.400.reduce_sub_computation | reduce | bytes 1310722
  296.9 7.4 %copy.147 = bf16[1,1280,256]{2,0,1:T(2,128)(2,1)S(1)} copy(bf16[1,1280,256]{2,1,0:T(8,128)(2,1)S(1)} %bitcast.545) | data formatting | bytes 1310720 | tf_op jit(solution)/shard_map/convert_element_type | solution.py:582
  304.3 6.9 %reduce.112 = bf16[1280,256]{1,0:T(8,128)(2,1)S(1)} reduce(bf16[1280,1,256]{2,1,0:T(2,128)(2,1)S(1)} %bitcast.532, bf16[]{:T(256)} %broadcast.1178), dimensions={1}, to_apply=%bitcast.399.reduce_sub_computation | reduce | bytes 1310722
  312.2 4.9 all-to-all-start.5
  322.1 8.5 %all-to-all-done.5 = bf16[4,2,40960]{2,1,0:T(2,128)(2,1)S(1)} async-done(((bf16[4,2,40960]{2,1,0:T(2,128)(2,1)}), bf16[4,2,40960]{2,1,0:T(2,128)(2,1)S(1)}, u32[]{:S(2)}, u32[]{:S(2)}) %all-to-all-start.5) | async-done | bytes 655392 | tf_op jit(solution)/shard_map/all_to_all | solution.py:581
  347.5 175.5 %shard_map.314 = (f32[128,1024]{1,0:T(8,128)}, f32[32,1024]{1,0:T(8,128)}, f32[32,4096]{1,0:T(8,128)}, f32[32,1024]{1,0:T(8,128)}, f32[32,1024]{1,0:T(8,128)}, /...) custom-call(bf16[320,4096]{1,0:T(8,128)(2,1)} %get-tuple-element.1029.refs_0_, ...), custom_call_target="tpu_custom_call" | custom-call | flops 8724152320 | bytes 31457280 | tf_op jit(solution)/shard_map/pallas_call | solution.py:427
  (605 shorter events, 199.4 us)
Async XLA Ops:
  0.7 8.1 %copy-start.34 = (f32[5,1024]{1,0:T(8,128)S(1)}, f32[5,1024]{1,0:T(8,128)}, u32[]{:S(2)}) copy-start(f32[5,1024]{1,0:T(8,128)} %param.32) | copy-start | bytes 61444
  0.7 9.4 %copy-start.37 = (bf16[1,1024]{1,0:T(2,128)(2,1)S(1)}, bf16[1,1024]{1,0:T(2,128)(2,1)}, u32[]{:S(2)}) copy-start(bf16[1,1024]{1,0:T(2,128)(2,1)} %param.25) | copy-start | bytes 6148
  3.9 6.2 %collective-permute-start = (bf16[1,1024]{1,0:T(2,128)(2,1)S(1)}, bf16[1,1024]{1,0:T(2,128)(2,1)S(1)}, u32[]{:S(2)}, u32[]{:S(2)}) collective-permute-start(bf16[1,1024]{1,0:T(2,128)(2,1)S(1)} %slice_bitcast_fusion.5), channel_id=1, source_target_pairs={{0,1},{1,2},{2,3},{4,5},{5,6},{6,7},{8,9},{9,10},{10,11},{12,13},{... | collective-permute-start | bytes 6152 | tf_op jit(solution)/shard_map/ppermute | solution.py:20
  25.9 6.0 %copy-start.9 = (bf16[320,1024]{1,0:T(8,128)(2,1)S(1)}, bf16[320,1024]{1,0:T(8,128)(2,1)}, u32[]{:S(2)}) copy-start(bf16[320,1024]{1,0:T(8,128)(2,1)} %get-tuple-element.1009.refs_5_) | copy-start | bytes 1966084
  25.9 22.1 %all-to-all-start = ((bf16[4,2,40960]{2,1,0:T(2,128)(2,1)}), bf16[4,2,40960]{2,1,0:T(2,128)(2,1)S(1)}, u32[]{:S(2)}, u32[]{:S(2)}) async-start(bf16[4,2,40960]{2,1,0:T(2,128)(2,1)} %reshape.1895), calls=%async_computation | async-start | bytes 1310720 | tf_op jit(solution)/shard_map/all_to_all | solution.py:504
  48.1 21.6 %all-to-all-start.1 = ((bf16[4,2,40960]{2,1,0:T(2,128)(2,1)}), bf16[4,2,40960]{2,1,0:T(2,128)(2,1)}, u32[]{:S(2)}, u32[]{:S(2)}) async-start(bf16[4,2,40960]{2,1,0:T(2,128)(2,1)} %reshape.1897), calls=%async_computation.1 | async-start | bytes 1310720 | tf_op jit(solution)/shard_map/all_to_all | solution.py:505
  104.9 14.3 %copy-start.21 = (f32[1,256]{1,0:T(1,128)}, f32[1,256]{1,0:T(1,128)S(1)}, u32[]{:S(2)}) copy-start(f32[1,256]{1,0:T(1,128)S(1)} %get-tuple-element.1476) | copy-start | bytes 3076
  105.0 14.3 %copy-start.28 = (f32[1,256]{1,0:T(1,128)}, f32[1,256]{1,0:T(1,128)S(1)}, u32[]{:S(2)}) copy-start(f32[1,256]{1,0:T(1,128)S(1)} %get-tuple-element.1475) | copy-start | bytes 3076
  105.0 14.3 %copy-start.30 = (f32[1,256]{1,0:T(1,128)}, f32[1,256]{1,0:T(1,128)S(1)}, u32[]{:S(2)}) copy-start(f32[1,256]{1,0:T(1,128)S(1)} %get-tuple-element.1474) | copy-start | bytes 3076
  140.4 9.4 %slice-start.2 = ((s8[8388608]{0:T(1024)(128)(4,1)}), s8[4194304]{0:T(1024)(128)(4,1)S(1)}, s32[]{:S(2)}) async-start(s8[8388608]{0:T(1024)(128)(4,1)} %bitcast.645), calls=%async_computation.8 | async-start | bytes 8388608
  142.1 7.8 %slice-start.3 = ((s8[8388608]{0:T(1024)(128)(4,1)}), s8[4194304]{0:T(1024)(128)(4,1)S(1)}, s32[]{:S(2)}) async-start(s8[8388608]{0:T(1024)(128)(4,1)} %bitcast.645), calls=%async_computation.9 | async-start | bytes 8388608
  145.4 3.4 collective-permute-start.1
  148.9 5.5 %slice-start = ((s8[8388608]{0:T(1024)(128)(4,1)}), s8[4194304]{0:T(1024)(128)(4,1)S(1)}, s32[]{:S(2)}) async-start(s8[8388608]{0:T(1024)(128)(4,1)} %bitcast.643), calls=%async_computation.6 | async-start | bytes 8388608
  149.8 9.4 %copy-start.13 = (bf16[320,1024]{1,0:T(8,128)(2,1)}, bf16[320,1024]{1,0:T(8,128)(2,1)S(1)}, u32[]{:S(2)}) copy-start(bf16[320,1024]{1,0:T(8,128)(2,1)S(1)} %get-tuple-element.1008.refs_1_) | copy-start | bytes 1966084
  154.4 4.9 copy-start.2
  161.7 14.5 %copy-start.18 = (bf16[320,1024]{1,0:T(8,128)(2,1)}, bf16[320,1024]{1,0:T(8,128)(2,1)S(1)}, u32[]{:S(2)}) copy-start(bf16[320,1024]{1,0:T(8,128)(2,1)S(1)} %get-tuple-element.1004.refs_8_) | copy-start | bytes 1966084
  178.2 5.8 %collective-permute-start.2 = (bf16[1,1024]{1,0:T(2,128)(2,1)S(1)}, bf16[1,1024]{1,0:T(2,128)(2,1)S(1)}, u32[]{:S(2)}, u32[]{:S(2)}) collective-permute-start(bf16[1,1024]{1,0:T(2,128)(2,1)S(1)} %slice_bitcast_fusion.3), channel_id=1, source_target_pairs={{1,0},{2,1},{3,2},{5,4},{6,5},{7,6},{9,8},{10,9},{11,10},{13,12},{... | collective-permute-start | bytes 6152 | tf_op jit(solution)/shard_map/ppermute | solution.py:20
  200.1 17.8 %all-to-all-start.3 = ((bf16[4,2,40960]{2,1,0:T(2,128)(2,1)}), bf16[4,2,40960]{2,1,0:T(2,128)(2,1)S(1)}, u32[]{:S(2)}, u32[]{:S(2)}) async-start(bf16[4,2,40960]{2,1,0:T(2,128)(2,1)} %reshape.1901), calls=%async_computation.3 | async-start | bytes 1310720 | tf_op jit(solution)/shard_map/all_to_all | solution.py:569
  292.6 19.6 %all-to-all-start.4 = ((bf16[4,2,40960]{2,1,0:T(2,128)(2,1)}), bf16[4,2,40960]{2,1,0:T(2,128)(2,1)}, u32[]{:S(2)}, u32[]{:S(2)}) async-start(bf16[4,2,40960]{2,1,0:T(2,128)(2,1)} %reshape.1905), calls=%async_computation.4 | async-start | bytes 1310720 | tf_op jit(solution)/shard_map/all_to_all | solution.py:574
  312.2 18.5 %all-to-all-start.5 = ((bf16[4,2,40960]{2,1,0:T(2,128)(2,1)}), bf16[4,2,40960]{2,1,0:T(2,128)(2,1)S(1)}, u32[]{:S(2)}, u32[]{:S(2)}) async-start(bf16[4,2,40960]{2,1,0:T(2,128)(2,1)} %reshape.1903), calls=%async_computation.5 | async-start | bytes 1310720 | tf_op jit(solution)/shard_map/all_to_all | solution.py:581
  339.0 5.5 %collective-permute-start.3 = (bf16[1,1024]{1,0:T(2,128)(2,1)S(1)}, bf16[1,1024]{1,0:T(2,128)(2,1)S(1)}, u32[]{:S(2)}, u32[]{:S(2)}) collective-permute-start(bf16[1,1024]{1,0:T(2,128)(2,1)S(1)} %slice_bitcast_fusion.2), channel_id=1, source_target_pairs={{1,0},{2,1},{3,2},{5,4},{6,5},{7,6},{9,8},{10,9},{11,10},{13,12},{... | collective-permute-start | bytes 6152 | tf_op jit(solution)/shard_map/ppermute | solution.py:20
  525.8 5.0 copy-start.26
  525.8 5.7 %copy-start.25 = (f32[32,1024]{1,0:T(8,128)S(1)}, f32[32,1024]{1,0:T(8,128)}, u32[]{:S(2)}) copy-start(f32[32,1024]{1,0:T(8,128)} %get-tuple-element.1484) | copy-start | bytes 393220
  525.8 6.3 %copy-start.24 = (f32[32,1024]{1,0:T(8,128)S(1)}, f32[32,1024]{1,0:T(8,128)}, u32[]{:S(2)}) copy-start(f32[32,1024]{1,0:T(8,128)} %get-tuple-element.1485) | copy-start | bytes 393220
  (33 other events, 75.4 us)

commit v2 on v0

v2 whole, which is shorter than its diff:
```python
from functools import partial
from typing import Any, NamedTuple

import jax
import jax.numpy as jnp
from jax import lax
from jax.experimental import pallas as pl
from jax.experimental.pallas import tpu as pltpu
from jax.sharding import PartitionSpec as P

EMBED_SIZE = 1024
FF = 4096
VMEM_BYTES = 62 << 20
MESH = pl.DeviceIdType.MESH


class Plan:
    def __init__(self, count_seg, count_tok):
        self.count_seg, self.count_tok = count_seg, count_tok
        self.bits = count_seg.bit_length() - 1
        self.seg_rows = EMBED_SIZE // count_seg
        self.seg_rows_ff = FF // count_seg
        self.low_bits = max(0, (128 // self.seg_rows).bit_length() - 1)
        self.pair = self.low_bits
        self.rest = [b for b in range(self.bits) if b != self.pair]
        self.orders = (self.rest, self.rest[::-1])
        self.stages = len(self.rest)
        self.slots = 1 << self.stages
        self.rows = self.seg_rows // count_tok
        self.rows_ff = self.seg_rows_ff // count_tok
        self.tok_here = self.rows % 16 == 0

    def recv_offset(self, stage):
        return self.slots - (self.slots >> stage)

    def slot(self, order, relative):
        total = 0
        for place, bit in enumerate(order):
            total = total + relative[bit] * (1 << (self.stages - 1 - place))
        return total


def bit_of(value, bit):
    return lax.rem(lax.div(value, 1 << bit), 2)


def flip(value, bit):
    return value + (1 - 2 * bit_of(value, bit)) * (1 << bit)


def seg_block(plan, seg, relative):
    total = bit_of(seg, plan.pair) * (1 << plan.pair)
    for bit, rel in relative.items():
        own = bit_of(seg, bit)
        total = total + (own + rel - 2 * own * rel) * (1 << bit)
    return total


def combos(bits):
    for index in range(1 << len(bits)):
        yield {bit: (index >> place) & 1 for place, bit in enumerate(bits)}


def greet(plan, seg, tok):
    barrier = pltpu.get_barrier_semaphore()
    for bit in range(plan.bits):
        pl.semaphore_signal(
            barrier, inc=1, device_id={"seg": flip(seg, bit)}, device_id_type=MESH
        )
    for step in range(1, plan.count_tok):
        pl.semaphore_signal(
            barrier,
            inc=1,
            device_id={"tok": lax.rem(tok + step, plan.count_tok)},
            device_id_type=MESH,
        )
    pl.semaphore_wait(barrier, plan.bits + plan.count_tok - 1)


class Copies:
    def __init__(self, local_sems, send_sems, recv_sems):
        self.local_sems, self.send_sems, self.recv_sems = local_sems, send_sems, recv_sems
        self.locals, self.remotes, self.open = 0, 0, []

    def local(self, source, target):
        copy = pltpu.make_async_copy(source, target, self.local_sems.at[self.locals])
        self.locals += 1
        copy.start()
        self.open.append(copy)
        return copy

    def remote(self, source, target, device):
        copy = pltpu.make_async_remote_copy(
            src_ref=source,
            dst_ref=target,
            send_sem=self.send_sems.at[self.remotes],
            recv_sem=self.recv_sems.at[self.remotes],
            device_id=device,
            device_id_type=MESH,
        )
        self.remotes += 1
        copy.start()
        self.open.append(copy)
        return copy

    def wait(self, *copies):
        for copy in copies:
            copy.wait()
            self.open = [item for item in self.open if item is not copy]

    def drain(self):
        self.wait(*list(self.open))


def rows16(index):
    return pl.ds(pl.multiple_of(index * 16, 16), 16)


def rows8(index):
    return pl.ds(pl.multiple_of(index * 8, 8), 8)


LANES = EMBED_SIZE // 128


def put_rows(staged, place, value):
    for block in range(LANES):
        staged[block, place] = value[:, 128 * block : 128 * block + 128]


def get_rows(staged, place):
    return jnp.concatenate([staged[block, place] for block in range(LANES)], axis=1)


def low(value):
    return value.astype(jnp.bfloat16).astype(jnp.float32)


def layer_norm(values, gain_row, bias_row):
    centre = values - jnp.mean(values, axis=-1, keepdims=True)
    spread = jnp.mean(centre * centre, axis=-1, keepdims=True)
    return centre * lax.rsqrt(spread + 1e-05) * gain_row + bias_row


def sweep(count, body, unroll=2):
    def step(index, carry):
        body(index)
        return carry

    lax.fori_loop(0, count, step, 0, unroll=unroll)


def matmul(left, right):
    return jnp.dot(left, right, preferred_element_type=jnp.float32)


def matmul_back(left, right):
    return lax.dot_general(
        left, right, (((1,), (1,)), ((), ())), preferred_element_type=jnp.float32
    )


def merge(state, later, faded):
    numer, denom, top = state
    reduced = top - faded
    peak = jnp.maximum(reduced, later[2])
    old, new = jnp.exp(reduced - peak), jnp.exp(later[2] - peak)
    return (old * numer + new * later[0], old * denom + new * later[1], peak)


def advance(state, key, value, fading):
    numer, denom, top = state
    reduced = top - fading
    peak = jnp.maximum(reduced, key)
    old, new = jnp.exp(reduced - peak), jnp.exp(key - peak)
    return (old * numer + new * value, old * denom + new, peak)


def row_of(state, index):
    return tuple(item[index : index + 1] for item in state)


def stack_rows(states):
    return tuple(jnp.concatenate([state[part] for state in states]) for part in range(len(states[0])))


def first_before(lead_row, last_tile):
    return jnp.concatenate([lead_row, last_tile[0:7]])


class ForwardRefs(NamedTuple):
    x: Any
    up: Any
    prior_one: Any
    prior_two: Any
    open_num: Any
    open_den: Any
    open_top: Any
    scales: Any
    shifts: Any
    blends: Any
    speed: Any
    reward: Any
    wk: Any
    wv: Any
    wr: Any
    wo: Any
    wl: Any
    wp: Any
    wa: Any
    layer_out: Any
    final: Any
    cat_squared: Any
    cat_recept_two: Any
    cat_key_two: Any
    cat_weighted: Any
    cat_recept_mix: Any
    cat_value_mix: Any
    cat_key_mix: Any
    cat_carried: Any
    cat_gate: Any
    sq_out: Any
    out_kf: Any
    out_vf: Any
    out_recept: Any
    out_mixed: Any
    out_xp: Any
    out_middle: Any
    out_upf: Any
    out_nf: Any
    out_nf2: Any
    out_entry: Any
    xb: Any
    ub: Any
    xs: Any
    xp: Any
    nf: Any
    nf2: Any
    kf: Any
    vf: Any
    recept: Any
    mixed: Any
    middle: Any
    upf: Any
    gate: Any
    carried: Any
    key_mix: Any
    value_mix: Any
    recept_mix: Any
    weighted: Any
    key_two: Any
    recept_two: Any
    sq: Any
    gc: Any
    gg: Any
    vk: Any
    vv: Any
    vr: Any
    vo: Any
    vl: Any
    vp: Any
    va: Any
    row_out: Any
    row_in: Any
    row_two_out: Any
    row_two_in: Any
    state_out: Any
    state_in: Any
    entry: Any
    whole: Any
    local_sems: Any
    send_sems: Any
    recv_sems: Any


class ForwardOut(NamedTuple):
    layer_out: Any
    final: Any
    cat_squared: Any
    cat_recept_two: Any
    cat_key_two: Any
    cat_weighted: Any
    cat_recept_mix: Any
    cat_value_mix: Any
    cat_key_mix: Any
    cat_carried: Any
    cat_gate: Any
    sq_out: Any
    out_kf: Any
    out_vf: Any
    out_recept: Any
    out_mixed: Any
    out_xp: Any
    out_middle: Any
    out_upf: Any
    out_nf: Any
    out_nf2: Any
    out_entry: Any


def right_of(plan, tok):
    return {"tok": lax.rem(tok + 1, plan.count_tok)}


def left_of(plan, tok):
    return {"tok": lax.rem(tok + plan.count_tok - 1, plan.count_tok)}


def forward_kernel(plan, *refs):
    r = ForwardRefs(*refs)
    seg, tok = lax.axis_index("seg"), lax.axis_index("tok")
    tokens = r.xs.shape[1]
    steps = tokens // 8
    every = lambda i: pl.ds(i, 8, stride=steps)
    pairs = tokens // 16
    copies = Copies(r.local_sems, r.send_sems, r.recv_sems)
    load_x = copies.local(r.x, r.xb)
    load_k, load_v = copies.local(r.wk, r.vk), copies.local(r.wv, r.vv)
    load_r, load_o = copies.local(r.wr, r.vr), copies.local(r.wo, r.vo)
    load_a = copies.local(r.wa, r.va)
    load_up = copies.local(r.up, r.ub)
    load_l = [copies.local(r.wl.at[:, pl.ds(1024 * j, 1024)], r.vl.at[j]) for j in range(4)]
    load_p = [copies.local(r.wp.at[pl.ds(1024 * j, 1024)], r.vp.at[j]) for j in range(4)]
    greet(plan, seg, tok)
    partner = {"seg": flip(seg, plan.pair)}
    mine = bit_of(seg, plan.pair)

    def share(source, target, wide, at=0):
        count = source.shape[1] // (2 * wide)
        for pick in range(count):
            own = pl.ds(pl.multiple_of((2 * pick + mine) * wide, wide), wide)
            other = pl.ds(pl.multiple_of((2 * pick + 1 - mine) * wide, wide), wide)
            place = pl.ds((at + pick) * wide, wide)
            copies.local(source.at[:, own], target.at[pl.ds(0, tokens), place])
            copies.remote(source.at[:, other], target.at[pl.ds(tokens, tokens), place], partner)

    def both(source, target):
        copies.local(source, target.at[pl.ds(0, tokens)])
        copies.remote(source, target.at[pl.ds(tokens, tokens)], partner)

    wide = max(128, plan.seg_rows)

    copies.wait(load_x)

    def widen(i):
        put_rows(r.xs, rows16(i), r.xb[rows16(i)].astype(jnp.float32))

    sweep(pairs, widen)
    gain, bias = r.scales[0:1], r.shifts[0:1]

    def norm_one(i):
        tile = get_rows(r.xs, every(i))
        r.xp[rows8(i)] = tile
        r.nf[rows8(i + 1)] = low(layer_norm(tile, gain, bias))

    norm_one(steps - 1)
    r.row_out[...] = r.nf[pl.ds(8 * steps, 8)]
    row = copies.remote(r.row_out, r.row_in, right_of(plan, tok))
    sweep(steps - 1, norm_one, 3)
    copies.wait(row)
    lead = jnp.where(tok == 0, r.prior_one[...].astype(jnp.float32), r.row_in[7:8])
    r.nf[0:8] = first_before(lead, r.nf[pl.ds(8 * steps, 8)])

    def mix_one(i):
        before = r.nf[pl.ds(pl.multiple_of(i * 16, 16), 16)]
        normed = r.nf[pl.ds(pl.multiple_of(i * 16 + 8, 8), 16)]
        for place, target in enumerate((r.key_mix, r.value_mix, r.recept_mix)):
            weight = r.blends[place : place + 1]
            target[rows16(i)] = (normed * weight + before * (1.0 - weight)).astype(jnp.bfloat16)

    sweep(pairs, mix_one)
    share(r.key_mix, r.cat_key_mix, wide)
    share(r.value_mix, r.cat_value_mix, wide)
    share(r.recept_mix, r.cat_recept_mix, wide)
    copies.local(r.xp, r.out_xp)
    copies.local(r.nf, r.out_nf)
    copies.wait(load_k)
    r.kf[...] = low(matmul(r.key_mix[...], r.vk[...]))
    copies.wait(load_v)
    r.vf[...] = low(matmul(r.value_mix[...], r.vv[...]))
    copies.local(r.kf, r.out_kf)
    copies.local(r.vf, r.out_vf)

    fading_row = jnp.exp(r.speed[...])
    fading = jnp.broadcast_to(fading_row, (8, EMBED_SIZE))
    reward = jnp.broadcast_to(r.reward[...], (8, EMBED_SIZE))
    zero = jnp.zeros((8, EMBED_SIZE), jnp.float32)

    def alone(i, state):
        return advance(state, r.kf[rows8(i)], r.vf[rows8(i)], fading)

    stretches = lax.fori_loop(0, steps, alone, (zero, zero, zero - 1e30), unroll=2)
    stretch_fade = fading_row * steps
    total = row_of(stretches, 0)
    for j in range(1, 8):
        total = merge(total, row_of(stretches, j), stretch_fade)
    portion = EMBED_SIZE // plan.count_tok
    lanes = pl.ds(pl.multiple_of(tok * portion, portion), portion)
    r.state_out[...] = zero
    for part, opening in enumerate((r.open_num, r.open_den, r.open_top)):
        r.state_out[part : part + 1] = total[part]
        r.state_out[3 + part : 4 + part, lanes] = opening[...]
    sent = [
        copies.remote(
            r.state_out, r.state_in.at[tok], {"tok": lax.rem(tok + step, plan.count_tok)}
        )
        for step in range(1, plan.count_tok)
    ]
    r.state_in[tok] = r.state_out[...]
    copies.wait(load_r)
    r.recept[...] = jax.nn.sigmoid(matmul(r.recept_mix[...], r.vr[...]))
    copies.local(r.recept, r.out_recept)
    copies.wait(*sent)
    state = tuple(
        sum(r.state_in[z, 3 + part : 4 + part] for z in range(plan.count_tok)) for part in range(3)
    )
    entry = state
    for z in range(plan.count_tok):
        entry = tuple(jnp.where(tok == z, new, old) for new, old in zip(state, entry))
        later = tuple(r.state_in[z, part : part + 1] for part in range(3))
        state = merge(state, later, fading_row * tokens)
    r.whole[...] = zero
    for part in range(3):
        r.whole[part : part + 1] = state[part]
    r.final[...] = r.whole[:, lanes]
    entries = [entry]
    for j in range(7):
        entries.append(merge(entries[-1], row_of(stretches, j), stretch_fade))
    entries = stack_rows(entries)
    for part in range(3):
        r.entry[8 * part : 8 * part + 8] = entries[part]
    keep_entry = copies.local(r.entry, r.out_entry)

    def emit(state, i):
        key, value = r.kf[rows8(i)], r.vf[rows8(i)]
        present = reward + key
        peak = jnp.maximum(state[2], present)
        old, new = jnp.exp(state[2] - peak), jnp.exp(present - peak)
        result = (old * state[0] + new * value) / (old * state[1] + new)
        return advance(state, key, value, fading), low(result)

    def recur(i, state):
        state, one = emit(state, 2 * i)
        state, two = emit(state, 2 * i + 1)
        both_rows = jnp.concatenate([one, two])
        r.mixed[rows16(i)] = both_rows
        r.weighted[rows16(i)] = (r.recept[rows16(i)] * both_rows).astype(jnp.bfloat16)
        return state

    lax.fori_loop(0, pairs, recur, entries)
    share(r.weighted, r.cat_weighted, wide)
    copies.local(r.mixed, r.out_mixed)
    copies.wait(load_o)
    r.middle[...] = r.xp[...] + matmul(r.weighted[...], r.vo[...])
    copies.local(r.middle, r.out_middle)

    gain_two, bias_two = r.scales[1:2], r.shifts[1:2]

    def norm_two(i):
        r.nf2[rows8(i + 1)] = low(layer_norm(r.middle[rows8(i)], gain_two, bias_two))

    norm_two(steps - 1)
    r.row_two_out[...] = r.nf2[pl.ds(8 * steps, 8)]
    row = copies.remote(r.row_two_out, r.row_two_in, right_of(plan, tok))
    sweep(steps - 1, norm_two, 3)
    copies.wait(row)
    lead = jnp.where(tok == 0, r.prior_two[...].astype(jnp.float32), r.row_two_in[7:8])
    r.nf2[0:8] = first_before(lead, r.nf2[pl.ds(8 * steps, 8)])

    def mix_two(i):
        before = r.nf2[pl.ds(pl.multiple_of(i * 16, 16), 16)]
        normed = r.nf2[pl.ds(pl.multiple_of(i * 16 + 8, 8), 16)]
        for place, target in ((3, r.key_two), (4, r.recept_two)):
            weight = r.blends[place : place + 1]
            target[rows16(i)] = (normed * weight + before * (1.0 - weight)).astype(jnp.bfloat16)

    sweep(pairs, mix_two)
    share(r.key_two, r.cat_key_two, wide)
    share(r.recept_two, r.cat_recept_two, wide)
    copies.local(r.nf2, r.out_nf2)
    copies.wait(load_a)
    r.gate[...] = jax.nn.sigmoid(matmul(r.recept_two[...], r.va[...]))
    copies.wait(load_up)

    def widen_up(i):
        put_rows(r.xs, rows16(i), r.ub[rows16(i)].astype(jnp.float32))

    sweep(pairs, widen_up)

    def carried_slope(i):
        up = jnp.concatenate(
            [get_rows(r.xs, every(2 * i)), get_rows(r.xs, every(2 * i + 1))]
        )
        r.upf[rows16(i)] = up
        r.gc[rows16(i)] = (up * r.gate[rows16(i)]).astype(jnp.bfloat16)

    sweep(pairs, carried_slope)
    both(r.gc, r.cat_carried)
    copies.local(r.upf, r.out_upf)
    for j in range(4):
        copies.wait(load_l[j])
        hidden = jnp.maximum(matmul(r.key_two[...], r.vl[j]), 0.0)
        r.sq[j] = (hidden * hidden).astype(jnp.bfloat16)
        share(r.sq.at[j], r.cat_squared, 4 * wide, j)
    copies.local(r.sq, r.sq_out)
    for j in range(4):
        copies.wait(load_p[j])
        part = matmul(r.sq[j], r.vp[j])
        r.carried[...] = part if j == 0 else r.carried[...] + part

    def close(i):
        gate, carried = r.gate[rows16(i)], r.carried[rows16(i)]
        gated = gate * carried
        result = r.middle[rows16(i)] + gated
        r.gg[rows16(i)] = (r.upf[rows16(i)] * gated * (1.0 - gate)).astype(jnp.bfloat16)
        put_rows(r.xs, every(2 * i), result[0:8])
        put_rows(r.xs, every(2 * i + 1), result[8:16])

    sweep(pairs, close)
    both(r.gg, r.cat_gate)

    def narrow(i):
        r.layer_out[rows16(i)] = get_rows(r.xs, rows16(i)).astype(jnp.bfloat16)

    sweep(pairs, narrow)
    copies.drain()


def forward(plan, arrays, tokens):
    f32, b16 = jnp.float32, jnp.bfloat16
    wide, half = (tokens, EMBED_SIZE), EMBED_SIZE // 2
    anywhere, vmem = pl.BlockSpec(memory_space=pl.ANY), pl.BlockSpec(memory_space=pltpu.VMEM)
    sds = jax.ShapeDtypeStruct
    out_shape = [sds(wide, b16), sds((8, EMBED_SIZE // plan.count_tok), f32)]
    out_shape += [sds((2 * tokens, FF // 2), b16)] + [sds((2 * tokens, half), b16)] * 6
    out_shape += [sds((2 * tokens, EMBED_SIZE), b16)] * 2 + [sds((4,) + wide, b16)]
    out_shape += [sds(wide, f32)] * 7
    out_shape += [sds((tokens + 8, EMBED_SIZE), f32)] * 2 + [sds((24, EMBED_SIZE), f32)]
    weight = pltpu.VMEM((EMBED_SIZE, EMBED_SIZE), b16)
    tile = pltpu.VMEM((8, EMBED_SIZE), f32)
    scratch = [pltpu.VMEM(wide, b16)] * 2
    scratch += [pltpu.VMEM((LANES, tokens, 128), f32), pltpu.VMEM(wide, f32)]
    scratch += [pltpu.VMEM((tokens + 8, EMBED_SIZE), f32)] * 2 + [pltpu.VMEM(wide, f32)] * 8
    scratch += [pltpu.VMEM(wide, b16)] * 6 + [pltpu.VMEM((4,) + wide, b16)]
    scratch += [pltpu.VMEM(wide, b16)] * 2 + [weight] * 4
    scratch += [pltpu.VMEM((4, EMBED_SIZE, EMBED_SIZE), b16)] * 2 + [weight]
    scratch += [tile] * 5 + [pltpu.VMEM((plan.count_tok, 8, EMBED_SIZE), f32)]
    scratch += [pltpu.VMEM((24, EMBED_SIZE), f32), tile]
    scratch += [pltpu.SemaphoreType.DMA((80,))] * 3
    got = pl.pallas_call(
        partial(forward_kernel, plan),
        out_shape=out_shape,
        in_specs=[anywhere] * 2 + [vmem] * 10 + [anywhere] * 7,
        out_specs=[vmem] * 2 + [anywhere] * (len(out_shape) - 2),
        scratch_shapes=scratch,
        compiler_params=pltpu.CompilerParams(
            collective_id=0, has_side_effects=True, vmem_limit_bytes=VMEM_BYTES
        ),
    )(*arrays)
    return ForwardOut(*got)


class Chunk:
    def __init__(self, number, ref, lane, wide, unit, share, out, column):
        self.number, self.ref, self.lane, self.wide = number, ref, lane, wide
        self.unit, self.share, self.out, self.column = unit, share, out, column


class Wire:
    RATE = 92e3
    LAG = 1.5
    BACKLOG = 5.0

    def __init__(self, plan, seg, tok, sems, far_sems):
        self.plan, self.seg, self.tok = plan, seg, tok
        self.send_sem, self.recv_sem = sems.at[0], sems.at[1]
        self.far_send, self.far_recv = far_sems.at[0], far_sems.at[1]
        self.clock, self.free = 0.0, {}
        self.waiting, self.flying = [], []

    def load(self, axis, amount):
        self.free[axis] = max(self.clock, self.free.get(axis, 0.0)) + amount / self.RATE
        return self.free[axis] + self.LAG

    def fly(self, arrival, action):
        self.flying.append((arrival, len(self.flying), action))

    def offer(self, chunk):
        self.waiting.append(chunk)
        self.serve()

    def tick(self, cost):
        self.clock += cost
        self.serve()

    def room(self):
        first = {order[0] for order in self.plan.orders}
        return min(self.free.get(axis, 0.0) for axis in first) - self.clock < self.BACKLOG

    def serve(self, rest=False):
        while self.flying or self.waiting:
            if self.waiting and self.room():
                self.start(self.waiting.pop(0))
                continue
            if not self.flying:
                break
            soonest = min(self.flying, key=lambda item: item[0])
            if soonest[0] > self.clock and not rest:
                break
            self.clock = max(self.clock, soonest[0])
            self.flying.remove(soonest)
            soonest[2]()

    def lanes(self, chunk, half):
        return pl.ds(chunk.lane + half * chunk.wide, chunk.wide)

    def recv_row(self, chunk, stage):
        return (self.plan.slots + self.plan.recv_offset(stage)) * chunk.unit

    def copy(self, chunk, half, stage):
        rows = (self.plan.slots >> (stage + 1)) * chunk.unit
        lanes = self.lanes(chunk, half)
        return pltpu.make_async_remote_copy(
            src_ref=chunk.ref.at[pl.ds(rows, rows), lanes],
            dst_ref=chunk.ref.at[pl.ds(self.recv_row(chunk, stage), rows), lanes],
            send_sem=self.send_sem.at[chunk.number, half, stage],
            recv_sem=self.recv_sem.at[chunk.number, half, stage],
            device_id={"seg": flip(self.seg, self.plan.orders[half][stage])},
            device_id_type=MESH,
        )

    def far_row(self, chunk, step):
        return (2 * self.plan.slots - 1) * chunk.unit + (step - 1) * chunk.share

    def far_copy(self, chunk, half, step):
        target = lax.rem(self.tok + step, self.plan.count_tok)
        lanes = self.lanes(chunk, half)
        start = pl.multiple_of(target * chunk.share, chunk.share)
        return pltpu.make_async_remote_copy(
            src_ref=chunk.ref.at[pl.ds(start, chunk.share), lanes],
            dst_ref=chunk.ref.at[pl.ds(self.far_row(chunk, step), chunk.share), lanes],
            send_sem=self.far_send.at[chunk.number, half, step - 1],
            recv_sem=self.far_recv.at[chunk.number, half, step - 1],
            device_id={"tok": target},
            device_id_type=MESH,
        )

    def start(self, chunk, stage=0):
        plan, arrivals = self.plan, [self.clock]
        for half in range(2):
            if stage < plan.stages:
                self.copy(chunk, half, stage).start()
                amount = (plan.slots >> (stage + 1)) * chunk.unit * chunk.wide * 4
                arrivals.append(self.load(plan.orders[half][stage], amount))
            elif plan.tok_here:
                for step in range(1, plan.count_tok):
                    self.far_copy(chunk, half, step).start()
                amount = chunk.share * chunk.wide * plan.count_tok * plan.count_tok
                arrivals.append(self.load(-1, amount))
        if stage < plan.stages:
            self.fly(max(arrivals), lambda: self.arrive(chunk, stage))
        else:
            self.fly(max(arrivals), lambda: self.finish(chunk))

    def arrive(self, chunk, stage):
        rows = (self.plan.slots >> (stage + 1)) * chunk.unit
        block = min(rows, 32768 // chunk.wide)
        for half in range(2):
            self.copy(chunk, half, stage).wait()
            lanes, base = self.lanes(chunk, half), self.recv_row(chunk, stage)

            def add(index):
                near = pl.ds(pl.multiple_of(index * block, block), block)
                came = pl.ds(pl.multiple_of(base + index * block, 16), block)
                total = chunk.ref[near, lanes].astype(jnp.float32)
                total = total + chunk.ref[came, lanes].astype(jnp.float32)
                chunk.ref[near, lanes] = total.astype(jnp.bfloat16)

            sweep(rows // block, add, 1)
        self.clock += 0.35 if stage == 0 else 0.2
        self.start(chunk, stage + 1)

    def finish(self, chunk):
        plan = self.plan
        for half in range(2):
            lanes = self.lanes(chunk, half)
            place = pl.ds(chunk.column + half * chunk.wide, chunk.wide)
            if not plan.tok_here:
                chunk.out[:, place] = chunk.ref[pl.ds(0, chunk.unit), lanes].astype(jnp.float32)
                continue
            mine = pl.ds(pl.multiple_of(self.tok * chunk.share, chunk.share), chunk.share)
            total = chunk.ref[mine, lanes].astype(jnp.float32)
            for step in range(1, plan.count_tok):
                self.far_copy(chunk, half, step).wait()
                came = pl.ds(self.far_row(chunk, step), chunk.share)
                total = total + chunk.ref[came, lanes].astype(jnp.float32)
            chunk.out[:, place] = total
        self.clock += 0.2


def outer_chunk(plan, seg, chunk, left, left_lane, right, right_lane):
    nsub = 1 << plan.low_bits
    high = [b for b in plan.rest if b >= plan.low_bits]
    columns = pl.ds(right_lane, 2 * chunk.wide)
    tall = chunk.unit == plan.seg_rows_ff
    for relative in combos(high):
        group = lax.div(lax.div(seg_block(plan, seg, relative), nsub), 2)
        span = chunk.unit if tall else chunk.unit * nsub
        for piece in range(nsub if tall else 1):
            index = group * nsub + piece if tall else group
            taken = left[:, pl.ds(pl.multiple_of(left_lane + index * span, 128), span)]
            result = lax.dot_general(
                taken,
                right[:, columns],
                (((0,), (0,)), ((), ())),
                preferred_element_type=jnp.float32,
            ).astype(jnp.bfloat16)
            for part in (piece,) if tall else range(nsub):
                full = dict(relative)
                for bit in range(plan.low_bits):
                    mine, want = bit_of(seg, bit), (part >> bit) & 1
                    full[bit] = mine + want - 2 * mine * want
                rows = result if tall else result[part * chunk.unit : (part + 1) * chunk.unit]
                for half in range(2):
                    slot = plan.slot(plan.orders[half], full)
                    start = slot * chunk.unit
                    if not isinstance(start, int):
                        start = pl.multiple_of(start, chunk.unit)
                    lanes = pl.ds(chunk.lane + half * chunk.wide, chunk.wide)
                    chunk.ref[pl.ds(start, chunk.unit), lanes] = rows[
                        :, half * chunk.wide : (half + 1) * chunk.wide
                    ]


def fold(value):
    return value[0:8] + value[8:16]


def total_rows(value):
    return jnp.sum(value, axis=0, keepdims=True)


def norm_back(values, slope, gain_row):
    centre = values - jnp.mean(values, axis=-1, keepdims=True)
    rate = lax.rsqrt(jnp.mean(centre * centre, axis=-1, keepdims=True) + 1e-05)
    scaled = centre * rate
    inner = slope * gain_row
    mean_inner = jnp.mean(inner, axis=-1, keepdims=True)
    mean_along = jnp.mean(inner * scaled, axis=-1, keepdims=True)
    return rate * (inner - mean_inner - scaled * mean_along), slope * scaled


class BackwardIn(NamedTuple):
    cat_squared: Any
    cat_recept_two: Any
    cat_key_two: Any
    cat_weighted: Any
    cat_recept_mix: Any
    cat_value_mix: Any
    cat_key_mix: Any
    cat_carried: Any
    cat_gate: Any
    sq_out: Any
    out_kf: Any
    out_vf: Any
    out_recept: Any
    out_mixed: Any
    out_xp: Any
    out_middle: Any
    out_upf: Any
    out_nf: Any
    out_nf2: Any
    entry: Any
    scales: Any
    blends: Any
    speed: Any
    reward: Any
    wk: Any
    wv: Any
    wr: Any
    wo: Any
    wl: Any
    wp: Any
    wa: Any


class BackwardOut(NamedTuple):
    token_grad: Any
    small: Any
    fvalue: Any
    frecept: Any
    fkey: Any
    aout: Any
    arecept: Any
    avalue: Any
    akey: Any


class BackwardRefs(NamedTuple):
    cat_squared: Any
    cat_recept_two: Any
    cat_key_two: Any
    cat_weighted: Any
    cat_recept_mix: Any
    cat_value_mix: Any
    cat_key_mix: Any
    cat_carried: Any
    cat_gate: Any
    sq_out: Any
    out_kf: Any
    out_vf: Any
    out_recept: Any
    out_mixed: Any
    out_xp: Any
    out_middle: Any
    out_upf: Any
    out_nf: Any
    out_nf2: Any
    entry: Any
    scales: Any
    blends: Any
    speed: Any
    reward: Any
    wk: Any
    wv: Any
    wr: Any
    wo: Any
    wl: Any
    wp: Any
    wa: Any
    token_grad: Any
    small: Any
    fvalue: Any
    frecept: Any
    fkey: Any
    aout: Any
    arecept: Any
    avalue: Any
    akey: Any
    vl: Any
    vp: Any
    va: Any
    early: Any
    tall: Any
    csq: Any
    cfr: Any
    cfk: Any
    gc: Any
    gg: Any
    gh: Any
    sqn: Any
    f0: Any
    f1: Any
    f2: Any
    f3: Any
    f4: Any
    f5: Any
    f6: Any
    row_out: Any
    row_in: Any
    row_one_out: Any
    row_one_in: Any
    state_out: Any
    state_in: Any
    small_in: Any
    sems: Any
    far_sems: Any
    local_sems: Any
    send_sems: Any
    recv_sems: Any
    ready: Any


def backward_kernel(plan, *refs):
    r = BackwardRefs(*refs)
    seg, tok = lax.axis_index("seg"), lax.axis_index("tok")
    tokens = r.sqn.shape[1]
    steps, pairs = tokens // 8, tokens // 16
    every = lambda i: pl.ds(i, 8, stride=steps)
    own_rows, pair_rows = pl.ds(0, tokens), pl.ds(tokens, tokens)
    partner = {"seg": flip(seg, plan.pair)}
    last_tok = plan.count_tok - 1
    copies = Copies(r.local_sems, r.send_sems, r.recv_sems)
    load = copies.local
    half = EMBED_SIZE // 2
    at_csq = load(r.cat_squared, r.csq)
    at_gc = load(r.cat_carried, r.gc)
    at_vp, at_sq = [None] * 4, [None] * 4
    for j in range(4):
        at_vp[j] = load(r.wp.at[pl.ds(1024 * j, 1024)], r.vp.at[j])
        if j < 2:
            at_sq[j] = load(r.sq_out.at[j], r.sqn.at[j])
    at_gg, at_cfr = load(r.cat_gate, r.gg), load(r.cat_recept_two, r.cfr)
    at_cfk = load(r.cat_key_two, r.cfk)
    at_vl = [load(r.wl.at[:, pl.ds(1024 * j, 1024)], r.vl.at[j]) for j in range(4)]
    at_va = load(r.wa, r.va)
    at_nf2 = load(r.out_nf2, r.f0)
    at_mid = load(r.out_middle, r.f1.at[own_rows])
    at_up = load(r.out_upf, r.f2.at[own_rows])
    at_rec = load(r.out_recept, r.f5.at[own_rows])
    greet(plan, seg, tok)
    wire = Wire(plan, seg, tok, r.sems, r.far_sems)

    share = plan.rows if plan.tok_here else 0
    share_ff = plan.rows_ff if plan.tok_here else 0
    tall = [
        Chunk(j, r.tall, 256 * j, 128, plan.seg_rows_ff, share_ff, r.fvalue, 256 * j)
        for j in range(4)
    ]
    flat = lambda number, ref, out, column: Chunk(
        number, ref, 0, half, plan.seg_rows, share, out, column
    )
    frecept = flat(4, r.early.at[0], r.frecept, 0)
    fkey = [flat(5 + j, r.early.at[1 + j], r.fkey, 1024 * j) for j in range(4)]
    late = [
        flat(9 + j, r.vl.at[j], out, 0)
        for j, out in enumerate((r.aout, r.arecept, r.avalue, r.akey))
    ]

    copies.wait(at_csq, at_gc)
    wire.clock = 4.0
    for j in range(4):
        outer_chunk(plan, seg, tall[j], r.csq, 0, r.gc, 256 * j)
        wire.clock += 1.1
        wire.offer(tall[j])
    cats = [
        load(cat, r.csq.at[:, pl.ds(half * j, half)])
        for j, cat in enumerate((r.cat_weighted, r.cat_recept_mix, r.cat_value_mix, r.cat_key_mix))
    ]
    sent = []
    for j in range(4):
        copies.wait(at_vp[j], at_sq[j])
        slope = matmul_back(r.gc[own_rows], r.vp[j])
        rate = 2.0 * jnp.sqrt(r.sqn[j % 2].astype(jnp.float32))
        r.gh[j, own_rows] = (slope * rate).astype(jnp.bfloat16)
        sent.append(copies.remote(r.gh.at[j, own_rows], r.gh.at[j, pair_rows], partner))
        if j < 2:
            at_sq[j + 2] = load(r.sq_out.at[j + 2], r.sqn.at[j])
        wire.tick(1.4)
    at_wo = load(r.wo, r.vp.at[3])
    at_wk, at_wv, at_wr = load(r.wk, r.vp.at[0]), load(r.wv, r.vp.at[1]), load(r.wr, r.vp.at[2])
    copies.wait(at_gg, at_cfr, at_cfk)
    outer_chunk(plan, seg, frecept, r.cfr, 0, r.gg, 0)
    wire.clock += 1.1
    wire.offer(frecept)
    for j in range(4):
        copies.wait(sent[j])
        outer_chunk(plan, seg, fkey[j], r.cfk, 0, r.gh.at[j], 0)
        wire.clock += 1.1
        wire.offer(fkey[j])
    for j in range(4):
        copies.wait(at_vl[j])
        part = matmul_back(r.gh[j, own_rows], r.vl[j])
        r.f3[own_rows] = part if j == 0 else r.f3[own_rows] + part
        wire.tick(1.1)
    copies.wait(at_va)
    r.f4[own_rows] = matmul_back(r.gg[own_rows], r.va[...])
    wire.tick(1.0)

    neighbours = [{"seg": flip(seg, bit)} for bit in range(plan.bits)]
    neighbours += [
        {"tok": lax.rem(tok + step, plan.count_tok)} for step in range(1, plan.count_tok)
    ]
    for device in neighbours:
        pl.semaphore_signal(r.ready, inc=1, device_id=device, device_id_type=MESH)

    def unmix(grads, weights, kept, row_out, row_in):
        def across(place):
            slopes = [grad[place] for grad in grads]
            total = slopes[0] * (1.0 - weights[0])
            for item, weight in zip(slopes[1:], weights[1:]):
                total = total + item * (1.0 - weight)
            return slopes, low(total)

        first = across(pl.ds(0, 8))[1]
        row_out[...] = first
        row = copies.remote(row_out, row_in, left_of(plan, tok))

        def step(i, sums):
            place = rows16(i)
            slopes, shifted = across(place)
            difference = kept[pl.ds(pl.multiple_of(16 * i + 8, 8), 16)] - kept[place]
            direct = slopes[0] * weights[0]
            for item, weight in zip(slopes[1:], weights[1:]):
                direct = direct + item * weight
            grads[0][place] = direct
            grads[-1][place] = shifted
            return tuple(fold(item * difference) + old for item, old in zip(slopes, sums))

        zero = jnp.zeros((8, EMBED_SIZE), jnp.float32)
        sums = lax.fori_loop(0, pairs, step, (zero,) * len(grads))
        copies.wait(row)
        end = jnp.where(tok == last_tok, 0.0, row_in[0:1])
        grads[-1][pl.ds(tokens, 8)] = jnp.concatenate([first[1:8], end])
        return [total_rows(item) for item in sums]

    def norm_pull(direct, shifted, values, gain_row, emit):
        def step(i, sums):
            place = rows16(i)
            slope = direct[place] + shifted[pl.ds(pl.multiple_of(16 * i + 8, 8), 16)]
            back, along = norm_back(values[place], slope, gain_row)
            emit(i, back)
            return fold(along) + sums[0], fold(slope) + sums[1]

        zero = jnp.zeros((8, EMBED_SIZE), jnp.float32)
        sums = lax.fori_loop(0, pairs, step, (zero, zero))
        return [total_rows(item) for item in sums]

    blend = lambda j: r.blends[j : j + 1]
    copies.wait(at_nf2)
    sums_two = unmix((r.f3, r.f4), (blend(3), blend(4)), r.f0, r.row_out, r.row_in)
    at_mixed = load(r.out_mixed, r.f0.at[own_rows])
    wire.tick(4.0)
    copies.wait(at_mid, at_up)

    def middle_slope(i, back):
        total = r.f2[rows16(i)] + back
        r.f2[rows16(i)] = total
        r.gh[0, rows16(i)] = total.astype(jnp.bfloat16)

    gain_two, bias_two = norm_pull(r.f3, r.f4, r.f1, r.scales[1:2], middle_slope)
    at_k = load(r.out_kf, r.f1.at[own_rows])
    at_v = load(r.out_vf, r.f4.at[own_rows])
    pl.semaphore_wait(r.ready, len(neighbours))
    to_pair = lambda j: copies.remote(r.gh.at[j, own_rows], r.gh.at[j, pair_rows], partner)
    pair_out = to_pair(0)
    wire.tick(4.0)
    copies.wait(at_wo)
    r.f3[own_rows] = matmul_back(r.gh[0, own_rows], r.vp[3])
    wire.tick(1.0)
    copies.wait(at_rec, at_mixed)

    def wkv_slope(i):
        place = rows16(i)
        slope, recept = r.f3[place], r.f5[place]
        gated = slope * recept
        r.f3[place] = low(gated)
        r.gh[1, place] = (gated * r.f0[place] * (1.0 - recept)).astype(jnp.bfloat16)

    sweep(pairs, wkv_slope)
    pair_recept = to_pair(1)
    wire.tick(1.5)
    copies.wait(pair_out, cats[0])
    outer_chunk(plan, seg, late[0], r.csq, 0, r.gh.at[0], 0)
    wire.clock += 1.1
    wire.offer(late[0])

    copies.wait(at_k, at_v)
    fading_row = jnp.exp(r.speed[...])
    fading = jnp.broadcast_to(fading_row, (8, EMBED_SIZE))
    reward = jnp.broadcast_to(r.reward[...], (8, EMBED_SIZE))
    zero = jnp.zeros((8, EMBED_SIZE), jnp.float32)
    key_ref, value_ref, slope_ref, top_ref, numer_ref, denom_ref = r.f1, r.f4, r.f3, r.f0, r.f5, r.f6

    def terms(state, key, value, slope):
        numer, denom, top = state
        present = reward + key
        peak = jnp.maximum(top, present)
        old, new = jnp.exp(top - peak), jnp.exp(present - peak)
        inverse = 1.0 / (old * denom + new)
        result = (old * numer + new * value) * inverse
        reduced = top - fading
        next_top = jnp.maximum(reduced, key)
        keep, put = jnp.exp(reduced - next_top), jnp.exp(key - next_top)
        scaled = slope * inverse
        return old * scaled, new * scaled, result, keep, put, next_top

    def onward(i, carry):
        numer, denom, top, alpha, beta, product = carry
        place = rows8(i)
        key, value = key_ref[place], value_ref[place]
        top_ref[place] = top
        numer_ref[place] = numer
        put_rows(denom_ref, place, denom)
        into, _, result, keep, put, next_top = terms((numer, denom, top), key, value, slope_ref[place])
        alpha = alpha + product * into
        beta = beta - product * into * result
        product = product * keep
        return keep * numer + put * value, keep * denom + put, next_top, alpha, beta, product

    entry = tuple(r.entry[8 * part : 8 * part + 8] for part in range(3))
    swept = lax.fori_loop(0, steps, onward, entry + (zero, zero, zero + 1.0))
    stretches = swept[3:]

    def pull_back(later, stretch):
        return (stretch[0] + stretch[2] * later[0], stretch[1] + stretch[2] * later[1])

    nothing = (jnp.zeros((1, EMBED_SIZE), jnp.float32),) * 2
    total, product = nothing, jnp.ones((1, EMBED_SIZE), jnp.float32)
    for j in range(7, -1, -1):
        total = pull_back(total, row_of(stretches, j))
        product = product * stretches[2][j : j + 1]
    r.state_out[...] = zero
    for part, item in enumerate(total + (product,)):
        r.state_out[part : part + 1] = item
    sent = [
        copies.remote(
            r.state_out, r.state_in.at[tok], {"tok": lax.rem(tok + step, plan.count_tok)}
        )
        for step in range(1, plan.count_tok)
    ]
    r.state_in[tok] = r.state_out[...]
    wire.tick(5.0)
    copies.wait(pair_recept, cats[1])
    outer_chunk(plan, seg, late[1], r.csq, half, r.gh.at[1], 0)
    wire.clock += 1.1
    wire.offer(late[1])
    copies.wait(*sent)
    later, entering = nothing, nothing
    for z in range(last_tok, -1, -1):
        entering = tuple(jnp.where(tok == z, new, old) for new, old in zip(later, entering))
        later = pull_back(later, tuple(r.state_in[z, part : part + 1] for part in range(3)))
    entries = [entering]
    for j in range(7, 0, -1):
        entries.insert(0, pull_back(entries[0], row_of(stretches, j)))
    entries = stack_rows(entries)

    def back(i, carry):
        alpha, beta, fade_sum, reward_sum = carry
        place = rows8(i)
        key, value, slope = key_ref[place], value_ref[place], slope_ref[place]
        numer, denom, top = numer_ref[place], get_rows(denom_ref, place), top_ref[place]
        into, now, result, keep, put, _ = terms((numer, denom, top), key, value, slope)
        reward_term = now * (value - result)
        key_slope = reward_term + put * (alpha * value + beta)
        value_slope = now + put * alpha
        fade_sum = fade_sum - keep * (alpha * numer + beta * denom)
        alpha, beta = keep * alpha + into, keep * beta - into * result
        return (alpha, beta, fade_sum, reward_sum + reward_term), key_slope, value_slope

    def backward_pair(index, carry):
        i = pairs - 1 - index
        carry, key_two, value_two = back(2 * i + 1, carry)
        carry, key_one, value_one = back(2 * i, carry)
        r.gh[2, rows16(i)] = jnp.concatenate([value_one, value_two]).astype(jnp.bfloat16)
        r.gh[3, rows16(i)] = jnp.concatenate([key_one, key_two]).astype(jnp.bfloat16)
        return carry

    _, _, fade_sum, reward_sum = lax.fori_loop(0, pairs, backward_pair, entries + (zero, zero))
    decay = total_rows(fade_sum) * fading_row
    bonus = total_rows(reward_sum)
    pair_value, pair_key = to_pair(2), to_pair(3)
    wire.tick(6.0)
    at_nf = load(r.out_nf, r.f4)
    at_xp = load(r.out_xp, r.f5.at[own_rows])
    copies.wait(at_wk)
    r.f0[own_rows] = matmul_back(r.gh[3, own_rows], r.vp[0])
    wire.tick(1.0)
    copies.wait(pair_value, cats[2])
    outer_chunk(plan, seg, late[2], r.csq, 2 * half, r.gh.at[2], 0)
    wire.clock += 1.1
    wire.offer(late[2])
    copies.wait(pair_key, cats[3])
    outer_chunk(plan, seg, late[3], r.csq, 3 * half, r.gh.at[3], 0)
    wire.clock += 1.1
    wire.offer(late[3])

    copies.wait(at_wv, at_wr)
    r.f1[own_rows] = matmul_back(r.gh[2, own_rows], r.vp[1])
    wire.tick(1.0)
    r.f3[own_rows] = matmul_back(r.gh[1, own_rows], r.vp[2])
    wire.tick(1.0)
    copies.wait(at_nf)
    sums_one = unmix(
        (r.f0, r.f1, r.f3),
        (blend(0), blend(1), blend(2)),
        r.f4,
        r.row_one_out,
        r.row_one_in,
    )
    wire.tick(4.5)
    copies.wait(at_xp)

    def input_slope(i, back):
        total = r.f2[rows16(i)] + back
        put_rows(r.f6, every(2 * i), total[0:8])
        put_rows(r.f6, every(2 * i + 1), total[8:16])

    gain_one, bias_one = norm_pull(r.f0, r.f3, r.f5, r.scales[0:1], input_slope)
    wire.tick(4.5)

    small_rows = [gain_one, gain_two, bias_one, bias_two] + sums_one + sums_two + [decay, bonus]
    r.small[...] = jnp.concatenate(
        small_rows + [jnp.zeros((16 - len(small_rows), EMBED_SIZE), jnp.float32)]
    )

    def small_stage(bit):
        copy = copies.remote(r.small, r.small_in.at[bit], {"seg": flip(seg, bit)})

        def next_stage():
            copies.wait(copy)
            r.small[...] += r.small_in[bit]
            if bit + 1 < plan.bits:
                small_stage(bit + 1)
            else:
                small_far()

        wire.fly(wire.clock + 4.0, next_stage)

    def small_far():
        base = plan.bits - 1
        sent = [
            copies.remote(
                r.small,
                r.small_in.at[base + step],
                {"tok": lax.rem(tok + step, plan.count_tok)},
            )
            for step in range(1, plan.count_tok)
        ]

        def end():
            copies.wait(*sent)
            total = r.small[...]
            for step in range(1, plan.count_tok):
                total = total + r.small_in[base + step]
            r.small[...] = total

        wire.fly(wire.clock + 6.0, end)

    small_stage(0)

    def narrow(i):
        r.token_grad[rows16(i)] = get_rows(r.f6, rows16(i)).astype(jnp.bfloat16)

    sweep(pairs, narrow)
    wire.serve(rest=True)
    copies.drain()


def backward(plan, arrays, tokens):
    f32, b16 = jnp.float32, jnp.bfloat16
    half = EMBED_SIZE // 2
    anywhere, vmem = pl.BlockSpec(memory_space=pl.ANY), pl.BlockSpec(memory_space=pltpu.VMEM)
    sds = jax.ShapeDtypeStruct
    far = plan.count_tok - 1
    rows = plan.rows if plan.tok_here else plan.seg_rows
    rows_ff = plan.rows_ff if plan.tok_here else plan.seg_rows_ff
    extra = far if plan.tok_here else 0
    out_shape = [sds((tokens, EMBED_SIZE), b16), sds((16, EMBED_SIZE), f32)]
    out_shape += [sds((rows_ff, EMBED_SIZE), f32), sds((rows, EMBED_SIZE), f32)]
    out_shape += [sds((rows, FF), f32)] + [sds((rows, EMBED_SIZE), f32)] * 4
    square = (4, EMBED_SIZE, EMBED_SIZE)
    held = (2 * plan.slots - 1) * plan.seg_rows + extra * plan.rows
    held_ff = (2 * plan.slots - 1) * plan.seg_rows_ff + extra * plan.rows_ff
    tile = pltpu.VMEM((8, EMBED_SIZE), f32)
    scratch = [pltpu.VMEM(square, b16)] * 2 + [pltpu.VMEM(square[1:], b16)]
    scratch += [pltpu.VMEM((5, held, EMBED_SIZE), b16), pltpu.VMEM((held_ff, EMBED_SIZE), b16)]
    scratch += [pltpu.VMEM((2 * tokens, FF // 2), b16)] + [pltpu.VMEM((2 * tokens, half), b16)] * 2
    scratch += [pltpu.VMEM((2 * tokens, EMBED_SIZE), b16)] * 2
    scratch += [pltpu.VMEM((4, 2 * tokens, EMBED_SIZE), b16), pltpu.VMEM((2, tokens, EMBED_SIZE), b16)]
    scratch += [pltpu.VMEM((tokens + 8, EMBED_SIZE), f32)] * 6
    scratch += [pltpu.VMEM((LANES, tokens, 128), f32)]
    scratch += [tile] * 5 + [pltpu.VMEM((plan.count_tok, 8, EMBED_SIZE), f32)]
    scratch += [pltpu.VMEM((plan.bits + far, 16, EMBED_SIZE), f32)]
    scratch += [pltpu.SemaphoreType.DMA((2, 13, 2, plan.stages)), pltpu.SemaphoreType.DMA((2, 13, 2, far))]
    scratch += [pltpu.SemaphoreType.DMA((80,))] * 3 + [pltpu.SemaphoreType.REGULAR]
    kinds = BackwardIn(*[anywhere] * len(arrays))
    kinds = kinds._replace(entry=vmem, scales=vmem, blends=vmem, speed=vmem, reward=vmem)
    got = pl.pallas_call(
        partial(backward_kernel, plan),
        out_shape=out_shape,
        in_specs=list(kinds),
        out_specs=[vmem] * len(out_shape),
        scratch_shapes=scratch,
        compiler_params=pltpu.CompilerParams(
            collective_id=1, has_side_effects=True, vmem_limit_bytes=VMEM_BYTES
        ),
    )(*arrays)
    return BackwardOut(*got)


def place_kernel(share, count, *refs):
    sources, finals, small = refs[:count], refs[count], refs[count + 1]
    targets, rest = refs[count + 2 : 2 * count + 2], refs[2 * count + 2 : -count - 1]
    held, sems = refs[-count - 1 : -1], refs[-1]
    into = [pltpu.make_async_copy(sources[i], held[i], sems.at[0, i]) for i in range(count)]
    away = [pltpu.make_async_copy(held[i], targets[i], sems.at[1, i]) for i in range(count)]
    for copy in into:
        copy.start()
    for part in range(3):
        rest[part][...] = finals[part : part + 1]
    device = lax.axis_index("seg") * lax.axis_size("tok") + lax.axis_index("tok")
    shift = lax.rem(EMBED_SIZE - device * share, EMBED_SIZE)
    turned = pltpu.roll(small[...], shift, 1)[:, :share]
    first = 0
    for target in rest[3:]:
        rows = target.shape[0]
        target[...] = turned[first : first + rows]
        first += rows
    for index in range(count):
        into[index].wait()
        away[index].start()
    for copy in away:
        copy.wait()


def place_results(plan, arrays, finals, small):
    share = EMBED_SIZE // (plan.count_seg * plan.count_tok)
    sds = jax.ShapeDtypeStruct
    anywhere, vmem = pl.BlockSpec(memory_space=pl.ANY), pl.BlockSpec(memory_space=pltpu.VMEM)
    count = len(arrays)
    small_shapes = [(1, finals.shape[1])] * 3 + [(2, share), (2, share), (5, share), (1, share), (1, share)]
    return pl.pallas_call(
        partial(place_kernel, share, count),
        out_shape=[sds(item.shape, item.dtype) for item in arrays]
        + [sds(shape, jnp.float32) for shape in small_shapes],
        in_specs=[anywhere] * count + [vmem] * 2,
        out_specs=[anywhere] * count + [vmem] * len(small_shapes),
        scratch_shapes=[pltpu.VMEM(item.shape, item.dtype) for item in arrays]
        + [pltpu.SemaphoreType.DMA((2, count))],
    )(*arrays, finals, small)


def shards(
    incoming_items,
    upstream_slope,
    timemix_prior_entry,
    featmix_prior_entry,
    opening_dividend,
    opening_divisor,
    opening_power,
    normalize_scales,
    normalize_shifts,
    shift_blends,
    logarithmic_fading_speed,
    present_reward,
    *weights,
):
    plan = Plan(lax.axis_size("seg"), lax.axis_size("tok"))
    tokens = incoming_items.shape[1]
    speed, reward = logarithmic_fading_speed[None], present_reward[None]
    ahead = forward(
        plan,
        (
            incoming_items[0],
            upstream_slope[0],
            timemix_prior_entry,
            featmix_prior_entry,
            opening_dividend,
            opening_divisor,
            opening_power,
            normalize_scales,
            normalize_shifts,
            shift_blends,
            speed,
            reward,
            *weights,
        ),
        tokens,
    )
    back = backward(
        plan,
        BackwardIn(*ahead[2:], normalize_scales, shift_blends, speed, reward, *weights),
        tokens,
    )
    sums = back[2:]
    if not plan.tok_here:
        sums = [lax.psum_scatter(item, "tok", scatter_dimension=0, tiled=True) for item in sums]
    placed = place_results(
        plan, [ahead.layer_out, back.token_grad, *sums], ahead.final, back.small
    )
    layer_out, token_grad, fvalue, frecept, fkey, aout, arecept, avalue, akey = placed[:9]
    numer, denom, top, gains, biases, mixes, decay, bonus = placed[9:]
    return (
        layer_out[None],
        token_grad[None],
        numer,
        denom,
        top,
        gains,
        biases,
        mixes,
        decay[0],
        bonus[0],
        akey,
        avalue,
        arecept,
        aout,
        fkey,
        fvalue,
        frecept,
    )


def solution(mesh):
    tokens, channels, whole = P("seg", "tok", None), P("seg", "tok"), P()
    spread, rows = P(None, ("seg", "tok")), P(("seg", "tok"), None)
    return jax.shard_map(
        shards,
        mesh=mesh,
        in_specs=(tokens,) * 2 + (P("seg", None),) * 2 + (channels,) * 3 + (whole,) * 12,
        out_specs=(tokens,) * 2
        + (channels,) * 3
        + (spread,) * 3
        + (P(("seg", "tok")),) * 2
        + (rows,) * 7,
        check_vma=False,
    )
```

time: 1710 us -> 184 us (0.11)
  waiting for transfers between devices: 1020 us -> 0 us
  local copies, waits for them, and re-layouts: 267 us -> 0 us
  Pallas kernels: 0 us -> 182 us
  other arithmetic: 135 us -> 0 us
  matrix products: 115 us -> 0 us
  blocking collectives: 113 us -> 0 us
  starting transfers between devices: 29.1 us -> 0 us
    reduce_scatter x7 -> x0, waiting for transfers between devices: 977 us -> none  [the longest x1 364 us: shards(): lax.psum_scatter(rows_for(grad_ffn_value, foremost_entries), ('seg', 'tok...]
    pallas_call x0 -> x3, Pallas kernels: none -> 182 us  [the longest x1 140 us: backward(): pl.pallas_call(partial(backward_kernel, plan), out_shape=out_shape, in_sp...]
    dot_general x81 -> x0, matrix products: 115 us -> none  [the longest x7 41.1 us: outer_sum(): lax.dot_general(left, right, (((0, 1), (0, 1)), ((), ())), preferred_elem...]
    reshape x19 -> x0, local copies, waits for them, and re-layouts: 84.8 us -> none  [the longest x7 66.8 us: rows_for(): return matrix.reshape(foremost_entries + (8, -1))]
    all_to_all x2 -> x0, blocking collectives: 62.2 us -> none  [the longest x1 31.3 us: shards(): lax.all_to_all(lookup_feature_slope.astype(jnp.bfloat16), 'tok', split_ax...]
    unnamed x1 -> x0, blocking collectives: 50.4 us -> none
    unnamed x12 -> x0, other arithmetic: 47.8 us -> none
    unnamed x178 -> x0, local copies, waits for them, and re-layouts: 46.2 us -> none
  transfers between devices with their start and end apart: 15 -> 0, of which waited for: 11 -> 0; matrix products, arithmetic and copies ran while one was open for 23% -> 0% of each run, Pallas kernels for 0% -> 0%
where the time goes in v2:
time: 184 us; the launch traced here: 183 us
  Pallas kernels  182 us (99%)
    pallas_call x1, Pallas kernels, backward(): pl.pallas_call(partial(backward_kernel, plan), out_shape=out_shape, in_sp...  140 us
    pallas_call x1, Pallas kernels, forward(): pl.pallas_call(partial(forward_kernel, plan), out_shape=out_shape, in_spe...  37.8 us
    pallas_call x1, Pallas kernels, place_results(): pl.pallas_call(partial(place_kernel, share, count), out_shape=[sds(item.s...  4.33 us

profile of v2, /device:TPU:0, one launch (start us, length us, event | category | flops | bytes accessed | tf_op | source)
XLA Modules:
  0.0 183.3 jit_solution(15564163131929296576)
XLA Ops:
  0.7 37.8 %shard_map.314 = (bf16[320,1024]{1,0:T(8,128)(2,1)}, f32[8,256]{1,0:T(8,128)}, bf16[640,2048]{1,0:T(8,128)(2,1)}, bf16[640,512]{1,0:T(8,128)(2,1)}, bf16[640,512...) custom-call(bf16[320,1024]{1,0:T(8,128)(2,1)} %bitcast.8, ...), custom_call_target="tpu_custom_call" | custom-call | tf_op jit(solution)/shard_map/pallas_call | solution.py:550
  38.4 140.3 %shard_map.315 = (bf16[320,1024]{1,0:T(8,128)(2,1)}, f32[16,1024]{1,0:T(8,128)}, f32[128,1024]{1,0:T(8,128)}, f32[32,1024]{1,0:T(8,128)}, f32[32,4096]{1,0:T(8,1...) custom-call(bf16[640,2048]{1,0:T(8,128)(2,1)} %get-tuple-element.66.refs_0_, ...), custom_call_target="tpu_custom_call" | custom-call | tf_op jit(solution)/shard_map/pallas_call | solution.py:1259
  178.8 4.3 %shard_map.316 = (bf16[320,1024]{1,0:T(8,128)(2,1)}, bf16[320,1024]{1,0:T(8,128)(2,1)}, f32[128,1024]{1,0:T(8,128)}, f32[32,1024]{1,0:T(8,128)}, f32[32,4096]{1,...) custom-call(bf16[320,1024]{1,0:T(8,128)(2,1)} %get-tuple-element.65., ...), custom_call_target="tpu_custom_call" | custom-call | tf_op jit(solution)/shard_map/pallas_call | solution.py:1303
